TPU v7x, 512 devices: a whole 4x4x16 slice. The times are simulated.
512 devices in a mesh: lon: 64 (over z_lo, y, core), lat: 8 (over z_hi, x).
Axes of the slice: x: 4, y: 4, z: 16 (z_hi: 2, z_lo: 8; z = z_hi * 8 + z_lo), core: 2. Of those that a mesh axis runs over, the one named last changes fastest.
Arguments:
- fields: bfloat16 [2, 48, 768, 192], P(None, 'lat', 'lon'), may hold values from -20 to 20
- cotangent: bfloat16 [2, 48, 768, 192], P(None, 'lat', 'lon'), may hold values from -6 to 6
- norm_gains: float32 [2, 192], replicated, may hold values from 0.1 to 1.9
- w_qkv: bfloat16 [2, 192, 576], replicated, may hold values from -0.4375 to 0.4375
- w_proj: bfloat16 [2, 192, 192], replicated, may hold values from -0.4375 to 0.4375
- tables: float32 [2, 8, 6, 3312], P(None, 'lat'), may hold values from -4 to 400
Outputs:
- block_out: bfloat16 [2, 48, 768, 192], P(None, 'lat', 'lon')
- grad_field: bfloat16 [2, 48, 768, 192], P(None, 'lat', 'lon')
- grad_gains: float32 [2, 192], replicated
- grad_qkv: float32 [2, 192, 576], replicated
- grad_proj: float32 [2, 192, 192], replicated
- grad_tables: float32 [2, 8, 6, 3312], P(None, 'lat')
All inputs are finite; a program needn't handle non-finite values.
Results may differ from a plain program's by a relative error of at most 0.013.
Values may be sent and summed in bfloat16 or wider, within the bound.
A program may use at most 64 MiB of HBM per device.

v0:
```python
import jax
import jax.numpy as jnp
from jax import lax
from jax.sharding import PartitionSpec as P

WLEV = 2
WLAT = 6
WLON = 12
WIN = 144
TAB = 3312


epsilon = 1e-05
highest = lax.Precision.HIGHEST


def from_behind(block, axis, distance):
    devices = range(lax.axis_size(axis))
    route = [((i - distance) % len(devices), i) for i in devices]
    return lax.ppermute(block, axis, route)


def to_windows(grid_in):
    levels, lat_rows, lon_cols, channels = grid_in.shape
    blocks = grid_in.reshape(
        levels // WLEV, WLEV, lat_rows // WLAT, WLAT, lon_cols // WLON, WLON, channels
    )
    blocks = blocks.transpose(2, 4, 0, 1, 3, 5, 6)
    return blocks.reshape(
        lat_rows // WLAT, lon_cols // WLON * (levels // WLEV), WLEV * WLAT * WLON, channels
    )


def from_windows(windowed, levels, lat_rows, lon_cols):
    channels = windowed.shape[-1]
    blocks = windowed.reshape(
        lat_rows // WLAT, lon_cols // WLON, levels // WLEV, WLEV, WLAT, WLON, channels
    )
    blocks = blocks.transpose(2, 3, 0, 4, 1, 5, 6)
    return blocks.reshape(levels, lat_rows, lon_cols, channels)


def offset_table():
    offset_span = 2 * WLON - 1
    query_lon = jnp.arange(WLON)[:, None]
    key_lon = jnp.arange(WLON)[None, :]
    offsets = (key_lon - query_lon + WLON - 1)[:, :, None]
    return (jnp.arange(offset_span)[None, None, :] == offsets).astype(jnp.float32)


def expand_bias(table):
    type_count, head_count = (table.shape[0], table.shape[1])
    shaped = table.reshape(type_count, head_count, WLEV, WLEV, WLAT, WLAT, 2 * WLON - 1)
    full_bias = jnp.einsum("thabcdr,qkr->thacqbdk", shaped, offset_table(), precision=highest)
    return full_bias.reshape(type_count, head_count, WIN, WIN)


def reduce_bias(full_grad):
    type_count, head_count = (full_grad.shape[0], full_grad.shape[1])
    shaped = full_grad.reshape(type_count, head_count, WLEV, WLAT, WLON, WLEV, WLAT, WLON)
    table = jnp.einsum("thacqbdk,qkr->thabcdr", shaped, offset_table(), precision=highest)
    return table.reshape(type_count, head_count, TAB)


def region_ids(levels, lat_pos, lat_total, lon_cols):
    level_pos = jnp.arange(levels)
    level_part = (level_pos >= levels - WLEV).astype(jnp.int32) + (
        level_pos >= levels - WLEV // 2
    ).astype(jnp.int32)
    lat_part = (lat_pos >= lat_total - WLAT).astype(jnp.int32) + (
        lat_pos >= lat_total - WLAT // 2
    ).astype(jnp.int32)
    labels = level_part[:, None] * 3 + lat_part[None, :]
    labels = jnp.broadcast_to(labels[:, :, None, None], (levels, lat_pos.shape[0], lon_cols, 1))
    return to_windows(labels)[..., 0]


def roll_field(grid_in, direction):
    half_lat = WLAT // 2
    half_lon = WLON // 2
    rolled = jnp.roll(grid_in, direction * (WLEV // 2), axis=0)
    if direction < 0:
        edge_rows, rest_rows = (rolled[:, :half_lat], rolled[:, half_lat:])
    else:
        edge_rows, rest_rows = (rolled[:, -half_lat:], rolled[:, :-half_lat])
    moved_rows = from_behind(edge_rows, "lat", direction)
    if direction < 0:
        rolled = jnp.concatenate([rest_rows, moved_rows], axis=1)
        edge_cols, rest_cols = (rolled[:, :, :half_lon], rolled[:, :, half_lon:])
    else:
        rolled = jnp.concatenate([moved_rows, rest_rows], axis=1)
        edge_cols, rest_cols = (rolled[:, :, -half_lon:], rolled[:, :, :-half_lon])
    moved_cols = from_behind(edge_cols, "lon", direction)
    if direction < 0:
        return jnp.concatenate([rest_cols, moved_cols], axis=2)
    return jnp.concatenate([moved_cols, rest_cols], axis=2)


def attn_probs(win_qkv, bias_full, labels):
    type_count, win_count, win_size, qkv_width = win_qkv.shape
    head_count = bias_full.shape[1]
    pieces = win_qkv.reshape(
        type_count, win_count, win_size, 3, head_count, qkv_width // (3 * head_count)
    )
    score_scale = pieces.shape[-1] ** (-0.5)
    scores = jnp.einsum(
        "aoqhe,aokhe->aohqk",
        pieces[:, :, :, 0],
        pieces[:, :, :, 1],
        preferred_element_type=jnp.float32,
    )
    scores = scores * score_scale + bias_full[:, None]
    if labels is not None:
        allowed = labels[:, :, None, :, None] == labels[:, :, None, None, :]
        scores = jnp.where(allowed, scores, -1e30)
    row_max = jnp.max(scores, axis=-1, keepdims=True)
    exp_scores = jnp.exp(scores - row_max)
    return (pieces, exp_scores / jnp.sum(exp_scores, axis=-1, keepdims=True))


def attention_forward(win_qkv, bias_full, labels):
    pieces, attn_p = attn_probs(win_qkv, bias_full, labels)
    probs_b = attn_p.astype(jnp.bfloat16)
    mixed_out = jnp.einsum(
        "aohqk,aokhe->aoqhe", probs_b, pieces[:, :, :, 2], preferred_element_type=jnp.float32
    )
    return mixed_out.reshape(win_qkv.shape[0], win_qkv.shape[1], win_qkv.shape[2], -1)


def attention_backward(win_qkv, bias_full, labels, grad_mixed):
    type_count, win_count, win_size = (win_qkv.shape[0], win_qkv.shape[1], win_qkv.shape[2])
    pieces, attn_p = attn_probs(win_qkv, bias_full, labels)
    head_count, head_dim = (pieces.shape[4], pieces.shape[5])
    score_scale = head_dim ** (-0.5)
    grad_heads = grad_mixed.reshape(type_count, win_count, win_size, head_count, head_dim)
    grad_probs = jnp.einsum(
        "aoqhe,aokhe->aohqk", grad_heads, pieces[:, :, :, 2], preferred_element_type=jnp.float32
    )
    grad_scores = attn_p * (grad_probs - jnp.sum(attn_p * grad_probs, axis=-1, keepdims=True))
    bias_grad = jnp.sum(grad_scores, axis=1)
    scores_b = grad_scores.astype(jnp.bfloat16)
    probs_b = attn_p.astype(jnp.bfloat16)
    grad_query = (
        jnp.einsum(
            "aohqk,aokhe->aoqhe", scores_b, pieces[:, :, :, 1], preferred_element_type=jnp.float32
        )
        * score_scale
    )
    grad_key = (
        jnp.einsum(
            "aohqk,aoqhe->aokhe", scores_b, pieces[:, :, :, 0], preferred_element_type=jnp.float32
        )
        * score_scale
    )
    grad_value = jnp.einsum(
        "aohqk,aoqhe->aokhe", probs_b, grad_heads, preferred_element_type=jnp.float32
    )
    grad_win = jnp.stack([grad_query, grad_key, grad_value], axis=3).astype(jnp.bfloat16)
    return (grad_win.reshape(type_count, win_count, win_size, -1), bias_grad)


def block_forward(grid_in, gain_vec, weight_qkv, weight_proj, bias_full, labels):
    levels, lat_rows, lon_cols, channels = grid_in.shape
    flat_rows = grid_in.reshape(-1, channels).astype(jnp.float32)
    centred = flat_rows - jnp.mean(flat_rows, axis=-1, keepdims=True)
    inv_std = lax.rsqrt(jnp.mean(centred * centred, axis=-1, keepdims=True) + epsilon)
    normed = centred * inv_std
    normed_b = (normed * gain_vec).astype(jnp.bfloat16)
    qkv_rows = jnp.dot(normed_b, weight_qkv, preferred_element_type=jnp.float32).astype(
        jnp.bfloat16
    )
    win_qkv = to_windows(qkv_rows.reshape(levels, lat_rows, lon_cols, 3 * channels))
    mixed_out = attention_forward(win_qkv, bias_full, labels).astype(jnp.bfloat16)
    merged = from_windows(mixed_out, levels, lat_rows, lon_cols).reshape(-1, channels)
    block_rows = flat_rows + jnp.dot(merged, weight_proj, preferred_element_type=jnp.float32)
    return (
        block_rows.astype(jnp.bfloat16).reshape(grid_in.shape),
        (normed, inv_std, normed_b, win_qkv, merged),
    )


def block_backward(saved, grad_out, gain_vec, weight_qkv, weight_proj, bias_full, labels):
    normed, inv_std, normed_b, win_qkv, merged = saved
    levels, lat_rows, lon_cols, channels = grad_out.shape
    grad_rows = grad_out.reshape(-1, channels)
    proj_sum = jnp.dot(merged.T, grad_rows, preferred_element_type=jnp.float32)
    grad_merged = jnp.dot(grad_rows, weight_proj.T, preferred_element_type=jnp.float32).astype(
        jnp.bfloat16
    )
    grad_windows = to_windows(grad_merged.reshape(levels, lat_rows, lon_cols, channels))
    grad_win_qkv, bias_sum = attention_backward(win_qkv, bias_full, labels, grad_windows)
    grad_qkv_rows = from_windows(grad_win_qkv, levels, lat_rows, lon_cols).reshape(-1, 3 * channels)
    qkv_sum = jnp.dot(normed_b.T, grad_qkv_rows, preferred_element_type=jnp.float32)
    grad_normed = jnp.dot(grad_qkv_rows, weight_qkv.T, preferred_element_type=jnp.float32)
    gain_sum = jnp.sum(grad_normed * normed, axis=0)
    grad_scaled = grad_normed * gain_vec
    grad_centre = grad_scaled - jnp.mean(grad_scaled, axis=-1, keepdims=True)
    grad_centre = grad_centre - normed * jnp.mean(grad_scaled * normed, axis=-1, keepdims=True)
    grad_in = (grad_rows.astype(jnp.float32) + inv_std * grad_centre).astype(jnp.bfloat16)
    return (grad_in.reshape(grad_out.shape), gain_sum, qkv_sum, proj_sum, reduce_bias(bias_sum))


def per_device(fields, cotangent, norm_gains, w_qkv, w_proj, tables):
    levels, lat_rows, lon_cols, channels = fields.shape
    lat_total = lat_rows * lax.axis_size("lat")
    lon_total = lon_cols * lax.axis_size("lon")
    lat_pos = lax.axis_index("lat") * lat_rows + jnp.arange(lat_rows)
    labels = region_ids(levels, lat_pos, lat_total, lon_cols)
    bias_first = expand_bias(tables[0])
    bias_second = expand_bias(tables[1])
    first_out, saved_first = block_forward(
        fields, norm_gains[0], w_qkv[0], w_proj[0], bias_first, None
    )
    shifted = roll_field(first_out, -1)
    second_out, saved_second = block_forward(
        shifted, norm_gains[1], w_qkv[1], w_proj[1], bias_second, labels
    )
    block_out = roll_field(second_out, 1)
    grad_second = roll_field(cotangent, -1)
    grad_shifted, gain_two, qkv_two, proj_two, table_two = block_backward(
        saved_second, grad_second, norm_gains[1], w_qkv[1], w_proj[1], bias_second, labels
    )
    grad_first = roll_field(grad_shifted, 1)
    grad_field, gain_one, qkv_one, proj_one, table_one = block_backward(
        saved_first, grad_first, norm_gains[0], w_qkv[0], w_proj[0], bias_first, None
    )
    gains_all, qkv_all, proj_all = lax.psum(
        (
            jnp.stack([gain_one, gain_two]),
            jnp.stack([qkv_one, qkv_two]),
            jnp.stack([proj_one, proj_two]),
        ),
        ("lon", "lat"),
    )
    tables_all = lax.psum(jnp.stack([table_one, table_two]), "lon")
    token_scale = float(levels * lat_total * lon_total) ** (-0.5)
    window_scale = float(lon_total // WLON) ** (-0.5)
    return (
        block_out,
        grad_field,
        gains_all * token_scale,
        qkv_all * token_scale,
        proj_all * token_scale,
        tables_all * window_scale,
    )


def solution(mesh):
    in_specs = (
        P(None, "lat", "lon", None),
        P(None, "lat", "lon", None),
        P(),
        P(),
        P(),
        P(None, "lat", None, None),
    )
    out_specs = (
        P(None, "lat", "lon", None),
        P(None, "lat", "lon", None),
        P(),
        P(),
        P(),
        P(None, "lat", None, None),
    )
    return jax.shard_map(
        per_device, mesh=mesh, in_specs=in_specs, out_specs=out_specs, check_vma=False
    )
```

profile of v0, /device:TPU:1, one launch (start us, length us, event | category | flops | bytes accessed | tf_op | source)
XLA Modules:
  0.0 1443.0 jit_solution(11559430177635052375)
XLA Ops:
  9.2 1.2 multiply_reduce_fusion.7
  10.4 1.3 fusion.82
  12.9 1.2 convolution_convert_fusion.1
  14.4 2.0 slice_reduce_fusion
  16.7 4.9 convolution_bitcast_fusion.1
  21.6 11.3 copy.212
  32.9 5.0 reshape.732
  40.3 18.5 %collective-permute-start = (bf16[2,3,12,192]{3,2,1,0:T(8,128)(2,1)S(1)}, bf16[2,3,12,192]{3,2,1,0:T(8,128)(2,1)S(1)}, u32[]{:S(2)}, u32[]{:S(2)}) collective-permute-start(bf16[2,3,12,192]{3,2,1,0:T(8,128)(2,1)S(1)} %get-tuple-element.53), channel_id=1, source_target_pairs={{1,0},{2,1},{3,2},{4,3},{5,4},{6,5},{7,6},{0,7},{9,8},{10,9},{11,1... | collective-permute-start | bytes 82952 | tf_op jit(solution)/shard_map/ppermute | solution.py:20
  60.6 2.5 collective-permute-start.4
  63.1 1.2 reshape.727
  65.3 5.6 convolution_bitcast_fusion
  71.2 11.3 copy.215
  82.5 5.0 reshape.734
  88.8 3.1 collective-permute-start.1
  92.0 1.5 fusion.66
  93.5 7.2 collective-permute-start.5
  102.3 1.3 fusion.11
  103.6 1.4 fusion.84
  106.6 1.6 reshape.715
  108.2 1.8 convolution_convert_fusion.7
  109.9 1.6 copy.178
  111.6 1.3 multiply_reduce_fusion.1
  112.9 1.3 subtract_multiply_fusion.1
  114.2 1.7 fusion.28
  115.9 1.8 fusion.27
  117.7 1.9 fusion.29
  119.5 1.3 rsqrt.26
  121.5 5.0 reshape.736
  126.5 1.3 convolution_convert_fusion.4
  128.7 1.7 convolution_bitcast_fusion.4
  131.5 2.0 convolution_bitcast_fusion.2
  133.5 1.1 fusion.24
  134.6 2.0 multiply_reduce_fusion.3
  137.5 2.8 collective-permute-start.6
  140.3 10.1 fusion.16
  152.9 1.9 collective-permute-start.2
  155.7 1.9 collective-permute-start.7
  157.6 11.0 collective-permute-done.2
  170.2 2.1 collective-permute-start.3
  174.1 5.0 reshape.735
  179.6 1.3 fusion.30
  180.9 10.2 fusion.13
  193.4 106.1 %psum.28 = f32[2,192]{1,0:T(2,128)S(1)} all-reduce(f32[2,192]{1,0:T(2,128)S(1)} %pad_maximum_fusion.13), channel_id=1, replica_groups=mesh['lon'=64,'lat'=8] {'lon','lat'}, use_global_device_ids=true, to_apply=%region_16.17 | all-reduce | flops 384 | bytes 3072 | tf_op jit(solution)/shard_map/psum | solution.py:227
  302.9 1.5 pad_maximum_fusion.8
  304.5 651.6 %all-reduce.4.cloned.1.call-done = f32[2,1,6,3312]{3,0,2,1:T(2,128)} async-done(((f32[2,1,6,3312]{3,0,2,1:T(2,128)}), f32[2,1,6,3312]{3,0,2,1:T(2,128)}) %all-reduce.4.cloned.1.call-update) | async-done | bytes 158992 | tf_op jit(solution)/shard_map/psum | solution.py:235
  957.8 474.3 %all-reduce.6.cloned.1.call-done = (f32[2,192,576]{2,1,0:T(8,128)}, f32[2,192,192]{2,1,0:T(8,128)}) async-done(((f32[2,192,576]{2,1,0:T(8,128)}, f32[2,192,192]{2,1,0:T(8,128)}), (f32[2,192,576]{2,1,0:T(8,128)}, f32[2,192,192]{2,1,0:T(8,128)})) %all-reduce.6.cloned.1.call-update) | async-done | bytes 1179664 | tf_op jit(solution)/shard_map/psum | solution.py:227
  1432.1 2.2 broadcast_multiply_fusion
  1434.3 1.8 broadcast_multiply_fusion.1
  (177 shorter events, 31.5 us)
Async XLA Ops:
  7.2 948.9 %all-reduce.4.cloned.1.call-start = ((), (), s32[]{:S(2)}) async-start(), calls=%async_computation | async-start | bytes 319488 | tf_op jit(solution)/shard_map/psum | solution.py:235
  11.7 21.2 %copy-start.28 = (f32[1,192]{1,0:T(1,128)}, f32[1,192]{1,0:T(1,128)S(1)}, u32[]{:S(2)}) copy-start(f32[1,192]{1,0:T(1,128)S(1)} %get-tuple-element.67) | copy-start | bytes 2308
  12.9 3.5 copy-start.13
  14.3 24.8 %copy-start.2 = (bf16[144,576]{0,1:T(8,128)(2,1)}, bf16[144,576]{0,1:T(8,128)(2,1)S(1)}, u32[]{:S(2)}) copy-start(bf16[144,576]{0,1:T(8,128)(2,1)S(1)} %copy.160) | copy-start | bytes 497668
  14.4 7.2 copy-start.21
  32.9 7.1 copy-start.10
  39.0 0.6 copy-start.25
  39.9 31.3 %copy-start.18 = (bf16[6,32,144]{2,1,0:T(8,128)(2,1)}, bf16[6,32,144]{2,1,0:T(8,128)(2,1)S(1)}, u32[]{:S(2)}) copy-start(bf16[6,32,144]{2,1,0:T(8,128)(2,1)S(1)} %convolution_convert_fusion.5) | copy-start | bytes 165892
  40.0 23.2 %copy-start.4 = (f32[144,192]{1,0:T(8,128)}, f32[144,192]{1,0:T(8,128)S(1)}, u32[]{:S(2)}) copy-start(f32[144,192]{1,0:T(8,128)S(1)} %reshape.722) | copy-start | bytes 331780
  40.3 48.5 %collective-permute-start = (bf16[2,3,12,192]{3,2,1,0:T(8,128)(2,1)S(1)}, bf16[2,3,12,192]{3,2,1,0:T(8,128)(2,1)S(1)}, u32[]{:S(2)}, u32[]{:S(2)}) collective-permute-start(bf16[2,3,12,192]{3,2,1,0:T(8,128)(2,1)S(1)} %get-tuple-element.53), channel_id=1, source_target_pairs={{1,0},{2,1},{3,2},{4,3},{5,4},{6,5},{7,6},{0,7},{9,8},{10,9},{11,1... | collective-permute-start | bytes 82952 | tf_op jit(solution)/shard_map/ppermute | solution.py:20
  60.6 31.3 %collective-permute-start.4 = (bf16[2,3,12,192]{3,0,2,1:T(2,128)(2,1)}, bf16[2,3,12,192]{3,0,2,1:T(2,128)(2,1)}, u32[]{:S(2)}, u32[]{:S(2)}) collective-permute-start(bf16[2,3,12,192]{3,0,2,1:T(2,128)(2,1)} %get-tuple-element.47), channel_id=1, source_target_pairs={{1,0},{2,1},{3,2},{4,3},{5,4},{6,5},{7,6},{0,7},{9,8},{10,9},{11,1... | collective-permute-start | bytes 82952 | tf_op jit(solution)/shard_map/ppermute | solution.py:20
  82.5 18.5 %copy-start.30 = (f32[1,192]{1,0:T(1,128)S(1)}, f32[1,192]{1,0:T(1,128)}, u32[]{:S(2)}) copy-start(f32[1,192]{1,0:T(1,128)} %get-tuple-element.66) | copy-start | bytes 2308
  82.5 18.7 %copy-start.16 = (bf16[2,192,576]{2,1,0:T(8,128)(2,1)S(1)}, bf16[2,192,576]{2,1,0:T(8,128)(2,1)}, u32[]{:S(2)}) copy-start(bf16[2,192,576]{2,1,0:T(8,128)(2,1)} %param.9) | copy-start | bytes 1327108
  88.8 13.5 copy-start.6
  88.8 11.8 collective-permute-start.1
  93.5 11.5 collective-permute-start.5
  100.7 1.7 copy-start.9
  101.0 1.3 copy-start.24
  101.2 1.1 copy-start.15
  105.0 7.9 copy-start
  121.5 5.0 copy-start.27
  126.5 10.1 copy-start.7
  126.5 10.1 copy-start.31
  126.5 10.1 copy-start.34
  126.5 10.1 copy-start.35
  131.5 41.8 %copy-start.11 = (bf16[2,192,192]{2,1,0:T(8,128)(2,1)S(1)}, bf16[2,192,192]{2,1,0:T(8,128)(2,1)}, u32[]{:S(2)}) copy-start(bf16[2,192,192]{2,1,0:T(8,128)(2,1)} %param.10) | copy-start | bytes 442372
  133.5 40.1 %copy-start.3 = (bf16[144,576]{0,1:T(8,128)(2,1)S(1)}, bf16[144,576]{0,1:T(8,128)(2,1)}, u32[]{:S(2)}) copy-start(bf16[144,576]{0,1:T(8,128)(2,1)} %copy-done.2) | copy-start | bytes 497668
  133.5 40.1 %copy-start.26 = (f32[6,144]{1,0:T(8,128)S(1)}, f32[6,144]{1,0:T(8,128)}, u32[]{:S(2)}) copy-start(f32[6,144]{1,0:T(8,128)} %copy-done.25) | copy-start | bytes 10372
  137.5 17.3 %collective-permute-start.6 = (bf16[2,3,12,192]{3,2,1,0:T(8,128)(2,1)}, bf16[2,3,12,192]{3,2,1,0:T(8,128)(2,1)}, u32[]{:S(2)}, u32[]{:S(2)}) collective-permute-start(bf16[2,3,12,192]{3,2,1,0:T(8,128)(2,1)} %get-tuple-element.48), channel_id=1, source_target_pairs={{7,0},{0,1},{1,2},{2,3},{3,4},{4,5},{5,6},{6,7},{15,8},{8,9},{9,10... | collective-permute-start | bytes 82952 | tf_op jit(solution)/shard_map/ppermute | solution.py:20
  150.5 0.6 copy-start.12
  152.9 15.7 %collective-permute-start.2 = (bf16[2,3,12,192]{3,0,2,1:T(2,128)(2,1)}, bf16[2,3,12,192]{3,0,2,1:T(2,128)(2,1)S(1)}, u32[]{:S(2)}, u32[]{:S(2)}) collective-permute-start(bf16[2,3,12,192]{3,0,2,1:T(2,128)(2,1)} %fusion.68), channel_id=1, source_target_pairs={{7,0},{0,1},{1,2},{2,3},{3,4},{4,5},{5,6},{6,7},{15,8},{8,9},{9,10... | collective-permute-start | bytes 82952 | tf_op jit(solution)/shard_map/ppermute | solution.py:20
  155.7 16.6 %collective-permute-start.7 = (bf16[2,6,6,192]{3,2,1,0:T(8,128)(2,1)S(1)}, bf16[2,6,6,192]{3,2,1,0:T(8,128)(2,1)S(1)}, u32[]{:S(2)}, u32[]{:S(2)}) collective-permute-start(bf16[2,6,6,192]{3,2,1,0:T(8,128)(2,1)S(1)} %fusion.64), channel_id=1, source_target_pairs={{504,0},{0,8},{8,16},{16,24},{24,32},{32,40},{40,48},{48,56},{56,6... | collective-permute-start | bytes 82952 | tf_op jit(solution)/shard_map/ppermute | solution.py:20
  170.2 132.7 %collective-permute-start.3 = (bf16[2,6,6,192]{3,0,2,1:T(2,128)(2,1)}, bf16[2,6,6,192]{3,0,2,1:T(2,128)(2,1)}, u32[]{:S(2)}, u32[]{:S(2)}) collective-permute-start(bf16[2,6,6,192]{3,0,2,1:T(2,128)(2,1)} %get-tuple-element.60), channel_id=1, source_target_pairs={{504,0},{0,8},{8,16},{16,24},{24,32},{32,40},{40,48},{48,56},{56,6... | collective-permute-start | bytes 82952 | tf_op jit(solution)/shard_map/ppermute | solution.py:20
  173.6 5.5 copy-start.23
  179.3 12.3 copy-start.20
  179.5 13.1 copy-start.14
  179.5 13.4 copy-start.5
  179.5 13.4 copy-start.17
  179.6 13.4 copy-start.29
  179.6 13.4 copy-start.32
  179.6 13.4 copy-start.33
  180.9 12.5 copy-start.36
  180.9 119.1 %copy-start.1 = (f32[1,192,576]{2,1,0:T(8,128)S(1)}, f32[1,192,576]{2,1,0:T(8,128)}, u32[]{:S(2)}) copy-start(f32[1,192,576]{2,1,0:T(8,128)} %convolution_bitcast_fusion.2) | copy-start | bytes 1327108
  180.9 120.3 %copy-start.19 = (bf16[6,32,144]{2,1,0:T(8,128)(2,1)S(1)}, bf16[6,32,144]{2,1,0:T(8,128)(2,1)}, u32[]{:S(2)}) copy-start(bf16[6,32,144]{2,1,0:T(8,128)(2,1)} %copy-done.18) | copy-start | bytes 165892
  180.9 120.5 %copy-start.8 = (f32[1,192,192]{2,1,0:T(8,128)S(1)}, f32[1,192,192]{2,1,0:T(8,128)}, u32[]{:S(2)}) copy-start(f32[1,192,192]{2,1,0:T(8,128)} %convolution_bitcast_fusion.4) | copy-start | bytes 442372
  180.9 122.0 %copy-start.22 = (bf16[2,6,6,192]{3,0,2,1:T(2,128)(2,1)S(1)}, bf16[2,6,6,192]{3,0,2,1:T(2,128)(2,1)}, u32[]{:S(2)}) copy-start(bf16[2,6,6,192]{3,0,2,1:T(2,128)(2,1)} %get-tuple-element.61) | copy-start | bytes 82948
  192.5 1239.7 %all-reduce.6.cloned.1.call-start = ((), (), s32[]{:S(2)}) async-start(), calls=%async_computation.1 | async-start | bytes 2752512 | tf_op jit(solution)/shard_map/psum | solution.py:227
Sparse Core Ops, SparseCore 0:
  192.6 763.4 all-reduce.3
  963.0 469.0 all-reduce.5
where the time goes:
time: 1450 us; the launch traced here: 1440 us
  waiting for transfers between devices  1140 us (79%)
  blocking collectives  106 us (7%)
  local copies, waits for them, and re-layouts  64.1 us (4%)
  matrix products  54 us (4%)
  starting transfers between devices  40.1 us (3%)
  other arithmetic  26.8 us (2%)
  between operations  15 us (1%)
    psum x1, waiting for transfers between devices, per_device(): tables_all = lax.psum(jnp.stack([table_one, table_two]), 'lon')  652 us
    psum x1, waiting for transfers between devices, per_device(): lax.psum((jnp.stack([gain_one, gain_two]), jnp.stack([qkv_one, qkv_two]),...  474 us
    psum x1, blocking collectives, per_device(): lax.psum((jnp.stack([gain_one, gain_two]), jnp.stack([qkv_one, qkv_two]),...  106 us
    ppermute x8, starting transfers between devices, from_behind(): return lax.ppermute(block, axis, route)  40 us
    another operation x4, local copies, waits for them, and re-layouts, attn_probs(): scores = scores * score_scale + bias_full[:, None]  32.6 us
  transfers between devices with their start and end apart: 10, of which 3 were waited for; matrix products, arithmetic and copies ran while one was open for 5% of the time, Pallas kernels for 0%

commit v1 on v0

v1 whole, which is shorter than its diff:
```python
import functools

import jax
import jax.numpy as jnp
from jax import lax
from jax.experimental import pallas as pl
from jax.experimental.pallas import tpu as pltpu
from jax.sharding import PartitionSpec as P

MESH = pl.DeviceIdType.MESH
ROWS = 192
QUAD = 48
C = 192
HEADS = 6
HD = 32
LAGS = 276
SCALE = HD**-0.5
epsilon = 1e-05
f32, bf16 = jnp.float32, jnp.bfloat16


def mm(a, b):
    return lax.dot_general(a, b, (((1,), (0,)), ((), ())), preferred_element_type=f32)


def mm_nt(a, b):
    return lax.dot_general(a, b, (((1,), (1,)), ((), ())), preferred_element_type=f32)


def mm_tn(a, b):
    return lax.dot_general(a, b, (((0,), (0,)), ((), ())), preferred_element_type=f32)


def row_parts(row):
    half = (row >= 96).astype(jnp.int32)
    lon = (row >> 3) - 12 * half
    slot = row & 7
    level = (slot >= 3).astype(jnp.int32)
    return half, lon, slot, level, slot - 3 * level


def iota(shape, dim):
    return lax.broadcasted_iota(jnp.int32, shape, dim)


def to_rows_matrix():
    half, lon, slot, level, lat = row_parts(iota((ROWS, 1), 0))
    source = (level * 6 + half * 3 + lat) * 16 + lon
    source = jnp.where(slot < 6, source, -1)
    return (iota((ROWS, ROWS), 1) == source).astype(f32).astype(bf16)


def from_rows_matrix():
    half, lon, slot, level, lat = row_parts(iota((1, ROWS), 1))
    target = (level * 6 + half * 3 + lat) * 16 + lon
    target = jnp.where(slot < 6, target, -1)
    return (iota((ROWS, ROWS), 0) == target).astype(f32).astype(bf16)


def load_grid(ref):
    grid = ref[...].astype(f32)
    grid = jnp.concatenate([grid, jnp.zeros((2, 6, 4, C), f32)], axis=2)
    return grid.reshape(ROWS, C).astype(bf16)


def store_grid(ref, rows):
    grid = rows.reshape(2, 6, 16, C)
    ref[...] = grid[:, :, :12, :].astype(bf16)


def build_lags(lag_ref):
    half, lon, slot, level, lat = row_parts(iota((ROWS, 1), 0))
    start = (level * 6 + half * 3 + lat) * 23 + lon + 11
    start = jnp.where(slot < 6, start, -100)
    lane = iota((ROWS, LAGS), 1)
    for o in range(12):
        lag_ref[o] = (lane == start - o).astype(f32).astype(bf16)


def expand(table, lag_ref, bias_ref, block, last):
    high = table.astype(bf16)
    rest = table - high.astype(f32)
    middle = rest.astype(bf16)
    low = (rest - middle.astype(f32)).astype(bf16)
    stacked = jnp.concatenate([high, middle, low], axis=0)
    khalf, _, kslot, klevel, _ = row_parts(iota((1, ROWS), 1))
    key_ok = kslot < 6
    if block:
        row = iota((96, 1), 0)
        slot = row & 7
        qhalf = (row >> 3) & 1
        qlevel = (slot >= 3).astype(jnp.int32)
        same_half = jnp.broadcast_to(qhalf, (96, ROWS)) == jnp.broadcast_to(khalf, (96, ROWS))
        same_level = jnp.broadcast_to(qlevel, (96, ROWS)) == jnp.broadcast_to(klevel, (96, ROWS))
        key_ok = key_ok & same_level & (same_half | jnp.logical_not(last))
    for o in range(12):
        parts = mm_nt(stacked, lag_ref[o])
        full = (parts[:96] + parts[96:192]) + parts[192:]
        full = jnp.where(key_ok, full, -1e30)
        bias_ref[block, :, :, o] = full.reshape(HEADS, 2, 8, ROWS)


def reduce_lags(gs_ref, lag_ref):
    total = jnp.zeros((96, LAGS), f32)
    for o in range(12):
        part = gs_ref[:, :, o].reshape(96, ROWS).astype(bf16)
        total = total + mm(part, lag_ref[o])
    return total


def head_mask(head):
    lane = iota((ROWS, C), 1)
    return (lane >= head * HD) & (lane < (head + 1) * HD)


def only(head, values):
    return jnp.where(head_mask(head), values, jnp.zeros_like(values))


def forward(block, rows_f, gain, w_qkv, w_proj, bias_ref, p_ref):
    centred = rows_f - jnp.mean(rows_f, axis=-1, keepdims=True)
    inv_std = lax.rsqrt(jnp.mean(centred * centred, axis=-1, keepdims=True) + epsilon)
    normed = centred * inv_std
    normed_b = (normed * gain).astype(bf16)
    q = mm(normed_b, w_qkv[:, :C]).astype(bf16)
    k = mm(normed_b, w_qkv[:, C : 2 * C]).astype(bf16)
    v = mm(normed_b, w_qkv[:, 2 * C :]).astype(bf16)
    mixed = jnp.zeros((ROWS, C), f32)
    for head in range(HEADS):
        bias = bias_ref[block, head].reshape(ROWS, ROWS)
        scores = mm_nt(only(head, q), k) * SCALE + bias
        exp_scores = jnp.exp(scores - jnp.max(scores, axis=-1, keepdims=True))
        probs = exp_scores / jnp.sum(exp_scores, axis=-1, keepdims=True)
        p_ref[block, head] = probs
        mixed = jnp.where(head_mask(head), mm(probs.astype(bf16), v), mixed)
    mixed_b = mixed.astype(bf16)
    result = rows_f + mm(mixed_b, w_proj)
    return result, (normed, inv_std, normed_b, q, k, v, mixed_b)


def backward(block, saved, grad_b, gain, w_qkv, w_proj, p_ref, gs_ref):
    normed, inv_std, normed_b, q, k, v, mixed_b = saved
    proj_sum = mm_tn(mixed_b, grad_b)
    grad_mixed = mm_nt(grad_b, w_proj).astype(bf16)
    grad_q = jnp.zeros((ROWS, C), f32)
    grad_k = jnp.zeros((ROWS, C), f32)
    grad_v = jnp.zeros((ROWS, C), f32)
    for head in range(HEADS):
        probs = p_ref[block, head]
        grad_head = only(head, grad_mixed)
        grad_probs = mm_nt(grad_head, v)
        weighted = jnp.sum(probs * grad_probs, axis=-1, keepdims=True)
        grad_scores = probs * (grad_probs - weighted)
        gs_ref[head] = grad_scores.reshape(2, 12, 8, ROWS)
        scores_b = grad_scores.astype(bf16)
        grad_q = jnp.where(head_mask(head), mm(scores_b, k), grad_q)
        grad_k = grad_k + mm_tn(scores_b, only(head, q))
        grad_v = grad_v + mm_tn(probs.astype(bf16), grad_head)
    grad_q = (grad_q * SCALE).astype(bf16)
    grad_k = (grad_k * SCALE).astype(bf16)
    grad_v = grad_v.astype(bf16)
    sums = jnp.concatenate(
        [mm_tn(normed_b, grad_q), mm_tn(normed_b, grad_k), mm_tn(normed_b, grad_v), proj_sum], axis=1
    )
    grad_normed = mm_nt(grad_q, w_qkv[:, :C]) + mm_nt(grad_k, w_qkv[:, C : 2 * C])
    grad_normed = grad_normed + mm_nt(grad_v, w_qkv[:, 2 * C :])
    gain_sum = jnp.sum(grad_normed * normed, axis=0, keepdims=True)
    grad_scaled = grad_normed * gain
    grad_centre = grad_scaled - jnp.mean(grad_scaled, axis=-1, keepdims=True)
    grad_centre = grad_centre - normed * jnp.mean(grad_scaled * normed, axis=-1, keepdims=True)
    grad_in = (grad_b.astype(f32) + inv_std * grad_centre).astype(bf16)
    return grad_in, gain_sum, sums


def place():
    lon, lat = lax.axis_index("lon"), lax.axis_index("lat")
    return dict(core=lon % 2, y=(lon // 2) % 4, z=(lat // 4) * 8 + lon // 8, x=lat % 4, lon=lon, lat=lat)


def device(core, y, z, x):
    return {"lon": ((z % 8) * 4 + y) * 2 + core, "lat": (z // 8) * 4 + x}


XY = [(dx, dy) for dx in range(4) for dy in range(4) if (dx, dy) != (0, 0)]


class Halo:
    def __init__(self, src, dst, send, recv, towards, sizes):
        self.src, self.dst, self.send, self.recv, self.towards = src, dst, send, recv, towards
        self.sizes = sizes

    def copies(self):
        me = place()
        n_lon, n_lat = self.sizes
        found = []
        for slot, (half, lon_half) in enumerate([(0, 0), (0, 1), (1, 0)]):
            if self.towards < 0:
                lat = (me["lat"] - (1 - half) + n_lat) % n_lat
                lon = (me["lon"] - (1 - lon_half) + n_lon) % n_lon
                source = (half, lon_half)
            else:
                lat = (me["lat"] + half_of(half)) % n_lat
                lon = (me["lon"] + half_of(lon_half)) % n_lon
                source = (1 - half, 1 - lon_half)
            start = source[0] * 96 + source[1] * QUAD
            end = (1 - source[0]) * 96 + (1 - source[1]) * QUAD
            found.append(
                pltpu.make_async_remote_copy(
                    src_ref=self.src.at[pl.ds(start, QUAD)],
                    dst_ref=self.dst.at[pl.ds(end, QUAD)],
                    send_sem=self.send.at[slot],
                    recv_sem=self.recv.at[slot],
                    device_id={"lon": lon, "lat": lat},
                    device_id_type=MESH,
                )
            )
        return found

    def start(self):
        for copy in self.copies():
            copy.start()
        own = 96 + QUAD if self.towards < 0 else 0
        there = 0 if self.towards < 0 else 96 + QUAD
        self.dst[there : there + QUAD] = self.src[own : own + QUAD]

    def finish(self):
        for copy in self.copies():
            copy.wait_recv()

    def drain(self):
        for copy in self.copies():
            copy.wait_send()


def half_of(half):
    return 1 - half


class Sums:
    def __init__(self, refs, send, recv):
        (self.w_src, self.t_src, self.w_core, self.t_core, self.w_xy, self.t_y, self.w_z, self.t_z,
         self.w_all, self.t_all) = refs
        self.send, self.recv = send, recv
        self.me = place()

    def copy(self, step, src, dst, to):
        copy = pltpu.make_async_remote_copy(
            src_ref=src, dst_ref=dst, send_sem=self.send.at[step], recv_sem=self.recv.at[step],
            device_id=to, device_id_type=MESH,
        )
        copy.start()

    def total(self, step):
        return {
            0: self.w_core, 1: self.t_core, 2: self.w_xy, 3: self.t_y, 4: self.w_xy, 5: self.t_z.at[pl.ds(0, 7)],
            6: self.w_xy, 7: self.t_y, 8: self.w_core, 9: self.t_core,
        }[step]

    def wait(self, step):
        pltpu.make_async_copy(self.total(step), self.total(step), self.recv.at[step]).wait()

    def drain(self):
        for step in range(10):
            pltpu.make_async_copy(self.total(step), self.total(step), self.send.at[step]).wait()

    def fill(self, sums, gains, table):
        for half in range(2):
            for tile in range(3):
                lanes = sums[:, (half * 3 + tile) * 128 : (half * 3 + tile + 1) * 128]
                self.w_src[half, 4 * tile : 4 * tile + 4] = lanes.reshape(4, 48, 128).astype(bf16)
            self.w_src[half, 12:16] = jnp.zeros((4, 48, 128), bf16)
        gains = jnp.concatenate([gains, jnp.zeros((1, 64), f32)], axis=1)
        gains = jnp.concatenate([gains[:, :128], gains[:, 128:], jnp.zeros((46, 128), f32)], axis=0)
        self.w_src[0, 12] = gains.astype(bf16)
        table = jnp.concatenate([table, jnp.zeros((96, 512 - LAGS), f32)], axis=1)
        for half in range(2):
            for tile in range(2):
                lanes = table[:, (half * 2 + tile) * 128 : (half * 2 + tile + 1) * 128]
                self.t_src[half, 2 * tile : 2 * tile + 2] = lanes.reshape(2, 48, 128).astype(bf16)

    def core_start(self):
        me = self.me
        other = 1 - me["core"]
        to = device(other, me["y"], me["z"], me["x"])
        self.copy(0, self.w_src.at[other], self.w_core, to)
        self.copy(1, self.t_src.at[other], self.t_core, to)

    def core_finish(self):
        me = self.me
        self.wait(0)
        self.w_core[...] = (self.w_src[me["core"]].astype(f32) + self.w_core[...].astype(f32)).astype(bf16)
        self.wait(1)
        self.t_core[...] = (self.t_src[me["core"]].astype(f32) + self.t_core[...].astype(f32)).astype(bf16)

    def xy_start(self):
        me = self.me
        for slot, (dx, dy) in enumerate(XY):
            x, y = (me["x"] + dx) % 4, (me["y"] + dy) % 4
            self.copy(2, self.w_core.at[y * 4 + x], self.w_xy.at[slot], device(me["core"], y, me["z"], x))
        for slot in range(3):
            y = (me["y"] + slot + 1) % 4
            self.copy(3, self.t_core.at[y], self.t_y.at[slot], device(me["core"], y, me["z"], me["x"]))

    def xy_finish(self):
        me = self.me
        self.wait(2)
        total = self.w_core[me["y"] * 4 + me["x"]].astype(f32)
        for slot in range(15):
            total = total + self.w_xy[slot].astype(f32)
        self.w_z[me["z"]] = total.astype(bf16)
        self.wait(3)
        total = self.t_core[me["y"]].astype(f32)
        for slot in range(3):
            total = total + self.t_y[slot].astype(f32)
        self.t_z[me["z"] % 8] = total.astype(bf16)

    def z_start(self):
        me = self.me
        for dz in (8, 7, 9, 6, 10, 5, 11, 4, 12, 3, 13, 2, 14, 1, 15):
            to = device(me["core"], me["y"], (me["z"] + dz) % 16, me["x"])
            self.copy(4, self.w_z.at[me["z"]], self.w_z.at[me["z"]], to)
        low = me["z"] % 8
        for dz in range(1, 8):
            to = device(me["core"], me["y"], me["z"] - low + (low + dz) % 8, me["x"])
            self.copy(5, self.t_z.at[low], self.t_z.at[low], to)

    def z_finish(self):
        me = self.me
        self.wait(4)
        total = self.w_z[0].astype(f32)
        for slot in range(1, 16):
            total = total + self.w_z[slot].astype(f32)
        self.w_all[me["core"], me["y"] * 4 + me["x"]] = total.astype(bf16)
        self.wait(5)
        total = self.t_z[0].astype(f32)
        for slot in range(1, 8):
            total = total + self.t_z[slot].astype(f32)
        self.t_all[me["core"], me["y"]] = total.astype(bf16)

    def back_start(self):
        me = self.me
        at = me["y"] * 4 + me["x"]
        for dx, dy in XY:
            to = device(me["core"], (me["y"] + dy) % 4, me["z"], (me["x"] + dx) % 4)
            self.copy(6, self.w_all.at[me["core"], at], self.w_all.at[me["core"], at], to)
        for dy in range(1, 4):
            to = device(me["core"], (me["y"] + dy) % 4, me["z"], me["x"])
            self.copy(7, self.t_all.at[me["core"], me["y"]], self.t_all.at[me["core"], me["y"]], to)

    def back_finish(self):
        self.wait(6)
        self.wait(7)

    def pair_start(self):
        me = self.me
        to = device(1 - me["core"], me["y"], me["z"], me["x"])
        self.copy(8, self.w_all.at[me["core"]], self.w_all.at[me["core"]], to)
        self.copy(9, self.t_all.at[me["core"]], self.t_all.at[me["core"]], to)

    def pair_finish(self, block, scale, table_scale, gains_ref, qkv_ref, proj_ref, table_ref):
        self.wait(8)
        self.wait(9)
        tiles = []
        for half in range(2):
            for tile in range(3):
                part = self.w_all[half, 4 * tile : 4 * tile + 4].astype(f32)
                tiles.append(part.reshape(ROWS, 128) * scale)
        for tile in range(4):
            qkv_ref[block, :, tile * 128 : (tile + 1) * 128] = tiles[tile]
        qkv_ref[block, :, 512:576] = tiles[4][:, :64]
        proj_ref[block] = jnp.concatenate([tiles[4][:, 64:], tiles[5]], axis=1)
        gains = self.w_all[0, 12].astype(f32) * scale
        gains_ref[block : block + 1, :128] = gains[0:1]
        gains_ref[block : block + 1, 128:] = gains[1:2, :64]
        for tile in range(3):
            part = self.t_all[tile // 2, 2 * (tile % 2) : 2 * (tile % 2) + 2].astype(f32)
            table_ref[block, :, tile * 128 : (tile + 1) * 128] = part.reshape(96, 128) * table_scale


def kernel(sizes, scale, table_scale, x_ref, ct_ref, gain_ref, w_qkv_ref, w_proj_ref, table_ref,
           out_ref, field_ref, gains_ref, qkv_ref, proj_ref, tables_ref,
           lag_ref, bias_ref, p_ref, gs_ref, halo_src, halo_dst, halo_send, halo_recv, *sum_refs):
    n_lon, n_lat = sizes
    alone = n_lon * n_lat == 1
    me = place()
    if not alone:
        barrier = pltpu.get_barrier_semaphore()
        count = 0
        for dlat, dlon in ((0, 1), (1, 0), (1, 1)):
            for sign in (1, -1):
                to = {"lon": (me["lon"] + sign * dlon + n_lon) % n_lon, "lat": (me["lat"] + sign * dlat + n_lat) % n_lat}
                pl.semaphore_signal(barrier, inc=1, device_id=to, device_id_type=MESH)
                count += 1
        partners = [device(1 - me["core"], me["y"], me["z"], me["x"])]
        partners += [device(me["core"], (me["y"] + dy) % 4, me["z"], (me["x"] + dx) % 4) for dx, dy in XY]
        partners += [device(me["core"], me["y"], (me["z"] + dz) % 16, me["x"]) for dz in range(1, 16)]
        for to in partners:
            pl.semaphore_signal(barrier, inc=1, device_id=to, device_id_type=MESH)
        count += len(partners)
    halos = [
        Halo(halo_src.at[n], halo_dst.at[n], halo_send.at[n], halo_recv.at[n], -1 if n < 2 else 1, sizes)
        for n in range(4)
    ]
    first, turned, second, back = halos

    def exchange(halo, rows):
        halo.src[...] = rows
        if alone:
            for half in range(2):
                for lon_half in range(2):
                    start = half * 96 + lon_half * QUAD
                    end = (1 - half) * 96 + (1 - lon_half) * QUAD
                    halo.dst[end : end + QUAD] = halo.src[start : start + QUAD]
        else:
            halo.start()

    def arrived(halo):
        if not alone:
            halo.finish()
        return halo.dst[...]

    last = me["lat"] == n_lat - 1
    to_rows = to_rows_matrix()
    from_rows = from_rows_matrix()
    x_rows = mm(to_rows, load_grid(x_ref))
    ct_rows = mm(to_rows, load_grid(ct_ref)).astype(bf16)
    build_lags(lag_ref)
    expand(table_ref[0], lag_ref, bias_ref, 0, last)
    gain = [gain_ref[0:1], gain_ref[1:2]]
    w_qkv = [w_qkv_ref[0], w_qkv_ref[1]]
    w_proj = [w_proj_ref[0], w_proj_ref[1]]
    first_out, saved_first = forward(0, x_rows, gain[0], w_qkv[0], w_proj[0], bias_ref, p_ref)
    if not alone:
        pl.semaphore_wait(barrier, count)
    exchange(first, first_out.astype(bf16))
    exchange(turned, ct_rows)
    expand(table_ref[1], lag_ref, bias_ref, 1, last)
    shifted = arrived(first).astype(f32)
    second_out, saved_second = forward(1, shifted, gain[1], w_qkv[1], w_proj[1], bias_ref, p_ref)
    exchange(second, second_out.astype(bf16))
    grad_second = arrived(turned)
    grad_shifted, gain_two, sums_two = backward(1, saved_second, grad_second, gain[1], w_qkv[1], w_proj[1], p_ref, gs_ref)
    exchange(back, grad_shifted)
    table_two = reduce_lags(gs_ref, lag_ref)
    if alone:
        grad_first = arrived(back)
        grad_field, gain_one, sums_one = backward(0, saved_first, grad_first, gain[0], w_qkv[0], w_proj[0], p_ref, gs_ref)
        table_one = reduce_lags(gs_ref, lag_ref)
        for block, (gains, sums, table) in enumerate(((gain_one, sums_one, table_one), (gain_two, sums_two, table_two))):
            gains_ref[block : block + 1] = gains * scale
            qkv_ref[block] = sums[:, :576] * scale
            proj_ref[block] = sums[:, 576:] * scale
            tables_ref[block, :, :LAGS] = table * table_scale
    else:
        outputs = (scale, table_scale, gains_ref, qkv_ref, proj_ref, tables_ref)
        half = len(sum_refs) // 2
        two = Sums(sum_refs[: half - 2], *sum_refs[half - 2 : half])
        one = Sums(sum_refs[half : 2 * half - 2], *sum_refs[2 * half - 2 :])
        two.fill(sums_two, gain_two, table_two)
        two.core_start()
        two.core_finish()
        two.xy_start()
        grad_first = arrived(back)
        grad_field, gain_one, sums_one = backward(0, saved_first, grad_first, gain[0], w_qkv[0], w_proj[0], p_ref, gs_ref)
        table_one = reduce_lags(gs_ref, lag_ref)
        one.fill(sums_one, gain_one, table_one)
        one.core_start()
        two.xy_finish()
        two.z_start()
        one.core_finish()
        one.xy_start()
    store_grid(field_ref, mm(from_rows, grad_field))
    store_grid(out_ref, mm(from_rows, arrived(second)))
    if not alone:
        one.xy_finish()
        one.z_start()
        two.z_finish()
        two.back_start()
        two.back_finish()
        two.pair_start()
        one.z_finish()
        one.back_start()
        two.pair_finish(1, *outputs)
        one.back_finish()
        one.pair_start()
        for halo in halos:
            halo.drain()
        two.drain()
        one.pair_finish(0, *outputs)
        one.drain()


def arrange(tables):
    shaped = tables[:, 0].reshape(2, HEADS, 2, 2, 2, 3, 6, 23)
    shaped = jnp.stack([shaped[0], shaped[1][:, ::-1, ::-1]])
    shaped = shaped.transpose(0, 1, 4, 2, 5, 3, 6, 7).reshape(2, HEADS * 2, 6, LAGS)
    return jnp.pad(shaped, ((0, 0), (0, 0), (0, 2), (0, 0))).reshape(2, 96, LAGS)


def restore(lagged):
    shaped = lagged[:, :, :LAGS].reshape(2, HEADS * 2, 8, LAGS)[:, :, :6]
    shaped = shaped.reshape(2, HEADS, 2, 2, 3, 2, 6, 23).transpose(0, 1, 3, 5, 2, 4, 6, 7)
    shaped = jnp.stack([shaped[0], shaped[1][:, ::-1, ::-1]])
    return shaped.reshape(2, 1, HEADS, 3312)


def per_device(fields, cotangent, norm_gains, w_qkv, w_proj, tables, *, sizes, interpret=False):
    n_lon, n_lat = sizes
    scale = float(2 * 6 * n_lat * 12 * n_lon) ** -0.5
    table_scale = float(n_lon) ** -0.5
    shapes = [
        jax.ShapeDtypeStruct(fields.shape, bf16),
        jax.ShapeDtypeStruct(fields.shape, bf16),
        jax.ShapeDtypeStruct((2, C), f32),
        jax.ShapeDtypeStruct((2, C, 3 * C), f32),
        jax.ShapeDtypeStruct((2, C, C), f32),
        jax.ShapeDtypeStruct((2, 96, 384), f32),
    ]
    vmem = pl.BlockSpec(memory_space=pltpu.VMEM)
    sum_scratch = [
        pltpu.VMEM((2, 16, 48, 128), bf16),
        pltpu.VMEM((2, 4, 48, 128), bf16),
        pltpu.VMEM((16, 48, 128), bf16),
        pltpu.VMEM((4, 48, 128), bf16),
        pltpu.VMEM((15, 48, 128), bf16),
        pltpu.VMEM((3, 48, 128), bf16),
        pltpu.VMEM((16, 48, 128), bf16),
        pltpu.VMEM((8, 48, 128), bf16),
        pltpu.VMEM((2, 16, 48, 128), bf16),
        pltpu.VMEM((2, 4, 48, 128), bf16),
        pltpu.SemaphoreType.DMA((10,)),
        pltpu.SemaphoreType.DMA((10,)),
    ]
    outs = pl.pallas_call(
        functools.partial(kernel, sizes, scale, table_scale),
        out_shape=shapes,
        in_specs=[vmem] * 6,
        out_specs=[vmem] * 6,
        scratch_shapes=[
            pltpu.VMEM((12, ROWS, LAGS), bf16),
            pltpu.VMEM((2, HEADS, 2, 12, 8, ROWS), f32),
            pltpu.VMEM((2, HEADS, ROWS, ROWS), f32),
            pltpu.VMEM((HEADS, 2, 12, 8, ROWS), f32),
            pltpu.VMEM((4, ROWS, C), bf16),
            pltpu.VMEM((4, ROWS, C), bf16),
            pltpu.SemaphoreType.DMA((4, 3)),
            pltpu.SemaphoreType.DMA((4, 3)),
        ]
        + (sum_scratch * 2 if n_lon * n_lat > 1 else []),
        compiler_params=pltpu.CompilerParams(
            collective_id=0 if n_lon * n_lat > 1 else None, has_side_effects=True, vmem_limit_bytes=56 * 2**20
        ),
        interpret=interpret,
    )(fields, cotangent, norm_gains, w_qkv, w_proj, arrange(tables))
    return (*outs[:5], restore(outs[5]))


def solution(mesh):
    grid = P(None, "lat", "lon", None)
    bands = P(None, "lat", None, None)
    sizes = (mesh.shape["lon"], mesh.shape["lat"])
    return jax.shard_map(
        functools.partial(per_device, sizes=sizes),
        mesh=mesh,
        in_specs=(grid, grid, P(), P(), P(), bands),
        out_specs=(grid, grid, P(), P(), P(), bands),
        check_vma=False,
    )
```

time: 1450 us -> 101 us (0.07)
  waiting for transfers between devices: 1140 us -> 0 us
  blocking collectives: 106 us -> 0 us
  Pallas kernels: 0 us -> 84.2 us
  matrix products: 54 us -> 0 us
  local copies, waits for them, and re-layouts: 64.1 us -> 15.7 us
  starting transfers between devices: 40.1 us -> 0 us
  other arithmetic: 26.8 us -> 0.3 us
    psum x2 -> x0, waiting for transfers between devices: 1130 us -> none  [the longest x1 652 us: per_device(): tables_all = lax.psum(jnp.stack([table_one, table_two]), 'lon')]
    psum x1 -> x0, blocking collectives: 106 us -> none  [per_device(): lax.psum((jnp.stack([gain_one, gain_two]), jnp.stack([qkv_one, qkv_two]),...]
    pallas_call x0 -> x1, Pallas kernels: none -> 84.2 us  [per_device(): pl.pallas_call(functools.partial(kernel, sizes, scale, table_scale), out_...]
    dot_general x28 -> x0, matrix products: 54 us -> none  [the longest x2 20.4 us: reduce_bias(): jnp.einsum('thacqbdk,qkr->thabcdr', shaped, offset_table(), precision=hig...]
    another operation x10 -> x3, local copies, waits for them, and re-layouts: 45.5 us -> 0.82 us  [the longest x2 0.77 us: restore(): shaped = jnp.stack([shaped[0], shaped[1][:, ::-1, ::-1]])]
    ppermute x8 -> x0, starting transfers between devices: 40 us -> none  [from_behind(): return lax.ppermute(block, axis, route)]
  transfers between devices with their start and end apart: 10 -> 0, of which waited for: 3 -> 0; matrix products, arithmetic and copies ran while one was open for 5% -> 0% of each run, Pallas kernels for 0% -> 0%
where the time goes in v1:
time: 101 us
  Pallas kernels  84.2 us (83%)
  local copies, waits for them, and re-layouts  15.7 us (16%)
    pallas_call x1, Pallas kernels, per_device(): pl.pallas_call(functools.partial(kernel, sizes, scale, table_scale), out_...  84.2 us
    unnamed x17, local copies, waits for them, and re-layouts  10.2 us

profile of v1, /device:TPU:1, one launch (start us, length us, event | category | flops | bytes accessed | tf_op | source)
XLA Modules:
  0.0 101.0 jit_solution(12783088756907545696)
XLA Ops:
  0.6 1.5 %copy.20.x_ref = bf16[2,6,12,192]{3,2,1,0:T(8,128)(2,1)} copy(bf16[2,6,12,192]{3,0,2,1:T(2,128)(2,1)} %param.6) | data formatting | bytes 110592 | tf_op args[0]
  2.2 1.5 %copy.21.ct_ref = bf16[2,6,12,192]{3,2,1,0:T(8,128)(2,1)} copy(bf16[2,6,12,192]{3,0,2,1:T(2,128)(2,1)} %param.7) | data formatting | bytes 110592 | tf_op args[1]
  3.7 1.3 %slice_reduce_fusion.1 = (f32[6,3312]{1,0:T(8,128)S(1)}, f32[6,3312]{1,0:T(8,128)S(1)}) fusion(f32[2,1,6,3312]{3,1,2,0:T(1,128)} %param.11), kind=kLoop, calls=%fused_computation.7 | loop fusion | bytes 317952 | tf_op jit(solution)/shard_map/slice | solution.py:495
  5.1 0.3 slice.23
  5.4 0.3 squeeze.6
  5.8 0.1 maximum_bitcast_fusion
  5.9 0.1 copy.31
  6.1 0.5 reshape.37
  6.6 0.7 pad_bitcast_fusion.table_ref
  7.3 84.2 %shard_map.109 = (bf16[2,6,12,192]{3,2,1,0:T(8,128)(2,1)}, bf16[2,6,12,192]{3,2,1,0:T(8,128)(2,1)}, f32[2,192]{1,0:T(2,128)}, f32[2,192,576]{2,1,0:T(8,128)}, f3...) custom-call(bf16[2,6,12,192]{3,2,1,0:T(8,128)(2,1)} %copy.20.x_ref, bf16[2,6,12,192]{3,2,1,0:T(8,128)(2,1)} %copy.21.ct_ref, ...), custom_call_target="tpu_custom_call" | custom-call | tf_op jit(solution)/shard_map/pallas_call | solution.py:534
  91.6 1.6 %copy.26 = bf16[2,6,12,192]{3,0,2,1:T(2,128)(2,1)} copy(bf16[2,6,12,192]{3,2,1,0:T(8,128)(2,1)} %get-tuple-element.24) | data formatting | bytes 110592
  93.2 1.6 %copy.27 = bf16[2,6,12,192]{3,0,2,1:T(2,128)(2,1)} copy(bf16[2,6,12,192]{3,2,1,0:T(8,128)(2,1)} %get-tuple-element.25) | data formatting | bytes 110592
  94.8 1.0 slice_bitcast_fusion.1
  95.8 0.2 copy.29
  95.9 0.6 reshape.34
  96.6 0.1 fusion
  96.7 0.1 copy.23
  96.8 0.4 stack.16
  97.2 0.0 copy-start.2
  97.3 0.0 copy-start
  97.3 0.1 copy.24
  97.3 0.4 stack.19
  97.7 0.1 pad_maximum_fusion
  97.9 0.0 copy-start.1
  97.9 0.8 copy.28
  98.7 0.0 copy-done.2
  98.7 0.6 copy.36
  99.3 0.0 copy-done
  99.3 0.9 copy.37
  100.2 0.0 copy-done.1
  100.2 0.7 copy.38
  (2 shorter events, 0.1 us)
Async XLA Ops:
  97.2 1.5 %copy-start.2 = (f32[2,192]{1,0:T(2,128)S(1)}, f32[2,192]{1,0:T(2,128)}, u32[]{:S(2)}) copy-start(f32[2,192]{1,0:T(2,128)} %get-tuple-element.42) | copy-start | bytes 4612
  97.3 2.0 %copy-start = (f32[2,192,576]{2,1,0:T(8,128)S(1)}, f32[2,192,576]{2,1,0:T(8,128)}, u32[]{:S(2)}) copy-start(f32[2,192,576]{2,1,0:T(8,128)} %get-tuple-element.43) | copy-start | bytes 2654212
  97.9 2.4 %copy-start.1 = (f32[2,192,192]{2,1,0:T(8,128)S(1)}, f32[2,192,192]{2,1,0:T(8,128)}, u32[]{:S(2)}) copy-start(f32[2,192,192]{2,1,0:T(8,128)} %get-tuple-element.44) | copy-start | bytes 884740

commit v2 on v1

v2 whole, which is shorter than its diff:
```python
import functools

import jax
import jax.numpy as jnp
from jax import lax
from jax.experimental import pallas as pl
from jax.experimental.pallas import tpu as pltpu
from jax.sharding import PartitionSpec as P

MESH = pl.DeviceIdType.MESH
ROWS = 192
WIN = 144
QUAD = 48
C = 192
HEADS = 6
HD = 32
LAGS = 276
TAB = 3312
SCALE = HD**-0.5
epsilon = 1e-05
f32, bf16 = jnp.float32, jnp.bfloat16


def mm(a, b):
    return lax.dot_general(a, b, (((1,), (0,)), ((), ())), preferred_element_type=f32)


def mm_nt(a, b):
    return lax.dot_general(a, b, (((1,), (1,)), ((), ())), preferred_element_type=f32)


def mm_tn(a, b):
    return lax.dot_general(a, b, (((0,), (0,)), ((), ())), preferred_element_type=f32)


def row_parts(row):
    half = (row >= 96).astype(jnp.int32)
    lon = (row >> 3) - 12 * half
    slot = row & 7
    level = (slot >= 3).astype(jnp.int32)
    return half, lon, slot, level, slot - 3 * level


def iota(shape, dim):
    return lax.broadcasted_iota(jnp.int32, shape, dim)


def to_rows_matrix():
    half, lon, slot, level, lat = row_parts(iota((ROWS, 1), 0))
    source = ((half * 3 + lat) * 12 + lon) * 2 + level
    source = jnp.where(slot < 6, source, -1)
    return (iota((ROWS, WIN), 1) == source).astype(f32).astype(bf16)


def from_rows_matrix():
    half, lon, slot, level, lat = row_parts(iota((1, ROWS), 1))
    target = ((half * 3 + lat) * 12 + lon) * 2 + level
    target = jnp.where(slot < 6, target, -1)
    return (iota((WIN, ROWS), 0) == target).astype(f32).astype(bf16)


def load_grid(ref):
    return ref[...].reshape(WIN, C)


def store_grid(ref, rows):
    ref[...] = rows.astype(bf16).reshape(6, 12, 2, C)


def build_lags(lag_ref):
    half, lon, slot, level, lat = row_parts(iota((ROWS, 1), 0))
    start = (level * 6 + half * 3 + lat) * 23 + lon + 11
    start = jnp.where(slot < 6, start, -100)
    lane = iota((ROWS, LAGS), 1)
    for o in range(12):
        lag_ref[o] = (lane == start - o).astype(f32).astype(bf16)


def table_places(block):
    for half in range(2):
        for slot in range(6):
            level, lat = slot // 3, 3 * half + slot % 3
            levels = [(level, 0), (level, 1)] if block == 0 else [(1 - level, 1), (1 - level, 0)]
            yield half, slot, [((a * 2 + b) * 6 + lat) * 138 for a, b in levels]


def expand(table_ref, flat_ref, lag_ref, bias_ref, block, last):
    flat = table_ref[block].reshape(HEADS, TAB)
    flat_ref[...] = jnp.zeros_like(flat_ref)
    for half, slot, starts in table_places(block):
        pieces = [flat[:, start : start + 138] for start in starts]
        flat_ref[:, half, slot, :] = jnp.concatenate(pieces, axis=1)
    table = flat_ref[...].reshape(96, LAGS)
    high = table.astype(bf16)
    rest = table - high.astype(f32)
    middle = rest.astype(bf16)
    low = (rest - middle.astype(f32)).astype(bf16)
    stacked = jnp.concatenate([high, middle, low], axis=0)
    khalf, _, kslot, klevel, _ = row_parts(iota((1, ROWS), 1))
    key_ok = kslot < 6
    if block:
        row = iota((96, 1), 0)
        slot = row & 7
        qhalf = (row >> 3) & 1
        qlevel = (slot >= 3).astype(jnp.int32)
        same_half = jnp.broadcast_to(qhalf, (96, ROWS)) == jnp.broadcast_to(khalf, (96, ROWS))
        same_level = jnp.broadcast_to(qlevel, (96, ROWS)) == jnp.broadcast_to(klevel, (96, ROWS))
        key_ok = key_ok & same_level & (same_half | jnp.logical_not(last))
    for o in range(12):
        parts = mm_nt(stacked, lag_ref[o])
        full = (parts[:96] + parts[96:192]) + parts[192:]
        full = jnp.where(key_ok, full, -1e30)
        bias_ref[block, :, :, o] = full.reshape(HEADS, 2, 8, ROWS)


def reduce_lags(gs_ref, lag_ref):
    total = jnp.zeros((96, LAGS), f32)
    for o in range(12):
        part = gs_ref[:, :, o].reshape(96, ROWS).astype(bf16)
        total = total + mm(part, lag_ref[o])
    return total


def dense_rows():
    row = iota((1, 96), 1)
    slot = row & 7
    target = (((row >> 3) & 1) * 6 + slot) * 6 + (row >> 4)
    target = jnp.where(slot < 6, target, -1)
    return (iota((80, 96), 0) == target).astype(f32).astype(bf16)


def head_mask(head):
    lane = iota((ROWS, C), 1)
    return (lane >= head * HD) & (lane < (head + 1) * HD)


def only(head, values):
    return jnp.where(head_mask(head), values, jnp.zeros_like(values))


def forward(block, rows_f, gain, w_qkv, w_proj, bias_ref, p_ref):
    centred = rows_f - jnp.mean(rows_f, axis=-1, keepdims=True)
    inv_std = lax.rsqrt(jnp.mean(centred * centred, axis=-1, keepdims=True) + epsilon)
    normed = centred * inv_std
    normed_b = (normed * gain).astype(bf16)
    q = mm(normed_b, w_qkv[:, :C]).astype(bf16)
    k = mm(normed_b, w_qkv[:, C : 2 * C]).astype(bf16)
    v = mm(normed_b, w_qkv[:, 2 * C :]).astype(bf16)
    mixed = jnp.zeros((ROWS, C), f32)
    for head in range(HEADS):
        bias = bias_ref[block, head].reshape(ROWS, ROWS)
        scores = mm_nt(only(head, q), k) * SCALE + bias
        exp_scores = jnp.exp(scores - jnp.max(scores, axis=-1, keepdims=True))
        probs = exp_scores / jnp.sum(exp_scores, axis=-1, keepdims=True)
        p_ref[block, head] = probs
        mixed = jnp.where(head_mask(head), mm(probs.astype(bf16), v), mixed)
    mixed_b = mixed.astype(bf16)
    result = rows_f + mm(mixed_b, w_proj)
    return result, (normed, inv_std, normed_b, q, k, v, mixed_b)


def backward(block, saved, grad_b, gain, w_qkv, w_proj, p_ref, gs_ref):
    normed, inv_std, normed_b, q, k, v, mixed_b = saved
    proj_sum = mm_tn(mixed_b, grad_b)
    grad_mixed = mm_nt(grad_b, w_proj).astype(bf16)
    grad_q = jnp.zeros((ROWS, C), f32)
    grad_k = jnp.zeros((ROWS, C), f32)
    grad_v = jnp.zeros((ROWS, C), f32)
    for head in range(HEADS):
        probs = p_ref[block, head]
        grad_head = only(head, grad_mixed)
        grad_probs = mm_nt(grad_head, v)
        weighted = jnp.sum(probs * grad_probs, axis=-1, keepdims=True)
        grad_scores = probs * (grad_probs - weighted)
        gs_ref[head] = grad_scores.reshape(2, 12, 8, ROWS)
        scores_b = grad_scores.astype(bf16)
        grad_q = jnp.where(head_mask(head), mm(scores_b, k), grad_q)
        grad_k = grad_k + mm_tn(scores_b, only(head, q))
        grad_v = grad_v + mm_tn(probs.astype(bf16), grad_head)
    grad_q = (grad_q * SCALE).astype(bf16)
    grad_k = (grad_k * SCALE).astype(bf16)
    grad_v = grad_v.astype(bf16)
    sums = jnp.concatenate(
        [mm_tn(normed_b, grad_q), mm_tn(normed_b, grad_k), mm_tn(normed_b, grad_v), proj_sum], axis=1
    )
    grad_normed = mm_nt(grad_q, w_qkv[:, :C]) + mm_nt(grad_k, w_qkv[:, C : 2 * C])
    grad_normed = grad_normed + mm_nt(grad_v, w_qkv[:, 2 * C :])
    gain_sum = jnp.sum(grad_normed * normed, axis=0, keepdims=True)
    grad_scaled = grad_normed * gain
    grad_centre = grad_scaled - jnp.mean(grad_scaled, axis=-1, keepdims=True)
    grad_centre = grad_centre - normed * jnp.mean(grad_scaled * normed, axis=-1, keepdims=True)
    grad_in = (grad_b.astype(f32) + inv_std * grad_centre).astype(bf16)
    return grad_in, gain_sum, sums


def place():
    lon, lat = lax.axis_index("lon"), lax.axis_index("lat")
    return dict(core=lon % 2, y=(lon // 2) % 4, z=(lat // 4) * 8 + lon // 8, x=lat % 4, lon=lon, lat=lat)


def device(core, y, z, x):
    return {"lon": ((z % 8) * 4 + y) * 2 + core, "lat": (z // 8) * 4 + x}


XY = [(dx, dy) for dx in range(4) for dy in range(4) if (dx, dy) != (0, 0)]


class Halo:
    def __init__(self, src, dst, send, recv, towards, sizes):
        self.src, self.dst, self.send, self.recv, self.towards = src, dst, send, recv, towards
        self.sizes = sizes

    def copies(self):
        me = place()
        n_lon, n_lat = self.sizes
        found = []
        for slot, (half, lon_half) in enumerate([(0, 0), (0, 1), (1, 0)]):
            if self.towards < 0:
                lat = (me["lat"] - (1 - half) + n_lat) % n_lat
                lon = (me["lon"] - (1 - lon_half) + n_lon) % n_lon
                source = (half, lon_half)
            else:
                lat = (me["lat"] + half_of(half)) % n_lat
                lon = (me["lon"] + half_of(lon_half)) % n_lon
                source = (1 - half, 1 - lon_half)
            start = source[0] * 96 + source[1] * QUAD
            end = (1 - source[0]) * 96 + (1 - source[1]) * QUAD
            found.append(
                pltpu.make_async_remote_copy(
                    src_ref=self.src.at[pl.ds(start, QUAD)],
                    dst_ref=self.dst.at[pl.ds(end, QUAD)],
                    send_sem=self.send.at[slot],
                    recv_sem=self.recv.at[slot],
                    device_id={"lon": lon, "lat": lat},
                    device_id_type=MESH,
                )
            )
        return found

    def start(self):
        for copy in self.copies():
            copy.start()
        own = 96 + QUAD if self.towards < 0 else 0
        there = 0 if self.towards < 0 else 96 + QUAD
        self.dst[there : there + QUAD] = self.src[own : own + QUAD]

    def finish(self):
        for copy in self.copies():
            copy.wait_recv()

    def drain(self):
        for copy in self.copies():
            copy.wait_send()


def half_of(half):
    return 1 - half


PLANE = [(dx, dy, dc) for dx in (2, 1, 3, 0) for dy in (2, 1, 3, 0) for dc in (1, 0) if (dx, dy, dc) != (0, 0, 0)]
YC = [(dy, dc) for dy in (2, 1, 3, 0) for dc in (1, 0) if (dy, dc) != (0, 0)]
FAR = (8, 7, 9, 6, 10, 5, 11, 4, 12, 3, 13, 2, 14, 1, 15)


def piece(index, rows):
    return pl.ds(pl.multiple_of(index * rows, rows), rows)


class Sums:
    def __init__(self, refs, send, recv):
        self.w_src, self.t_src, self.w_in, self.t_in, self.w_z, self.t_z, self.w_all, self.t_all = refs
        self.send, self.recv = send, recv
        self.me = me = place()
        self.w_at = (me["y"] * 4 + me["x"]) * 2 + me["core"]
        self.t_at = me["y"] * 2 + me["core"]

    def copy(self, step, src, dst, to):
        pltpu.make_async_remote_copy(
            src_ref=src, dst_ref=dst, send_sem=self.send.at[step], recv_sem=self.recv.at[step],
            device_id=to, device_id_type=MESH,
        ).start()

    def total(self, step):
        return (self.w_in, self.t_in, self.w_z.at[pl.ds(0, 15)], self.t_z.at[pl.ds(0, 7)], self.w_in, self.t_in)[step]

    def wait(self, step):
        pltpu.make_async_copy(self.total(step), self.total(step), self.recv.at[step]).wait()

    def drain(self):
        for step in range(6):
            pltpu.make_async_copy(self.total(step), self.total(step), self.send.at[step]).wait()

    def fill(self, sums, gains):
        for tile in range(6):
            lanes = sums[:, tile * 128 : (tile + 1) * 128]
            self.w_src[4 * tile : 4 * tile + 4] = lanes.reshape(4, 48, 128).astype(bf16)
        self.w_src[24:32] = jnp.zeros((8, 48, 128), bf16)
        gains = jnp.concatenate([gains, jnp.zeros((1, 64), f32)], axis=1)
        gains = jnp.concatenate([gains[:, :128], gains[:, 128:], jnp.zeros((46, 128), f32)], axis=0)
        self.w_src[24] = gains.astype(bf16)

    def fill_table(self, table):
        table = jnp.concatenate([table, jnp.zeros((96, 384 - LAGS), f32)], axis=1)
        table = mm(dense_rows(), table.astype(bf16)).astype(bf16)
        for tile in range(3):
            self.t_src[80 * tile : 80 * tile + 80] = table[:, tile * 128 : (tile + 1) * 128]
        self.t_src[240:256] = jnp.zeros((16, 128), bf16)

    def plane(self, dx, dy, dc):
        me = self.me
        x, y, core = (me["x"] + dx) % 4, (me["y"] + dy) % 4, (me["core"] + dc) % 2
        return (y * 4 + x) * 2 + core, y * 2 + core, device(core, y, me["z"], x)

    def scatter(self):
        for slot, offset in enumerate(PLANE):
            at, _, to = self.plane(*offset)
            self.copy(0, self.w_src.at[at], self.w_in.at[slot], to)

    def scatter_table(self):
        for slot, offset in enumerate(YC):
            _, at, to = self.plane(0, *offset)
            self.copy(1, self.t_src.at[piece(at, 32)], self.t_in.at[slot], to)

    def scattered(self):
        self.wait(0)
        total = self.w_src[self.w_at].astype(f32)
        for slot in range(31):
            total = total + self.w_in[slot].astype(f32)
        self.w_z[self.me["z"]] = total.astype(bf16)

    def scattered_table(self):
        self.wait(1)
        total = self.t_src[piece(self.t_at, 32)].astype(f32)
        for slot in range(7):
            total = total + self.t_in[slot].astype(f32)
        self.t_z[self.me["z"] % 8] = total.astype(bf16)

    def exchange(self):
        me = self.me
        for dz in FAR:
            to = device(me["core"], me["y"], (me["z"] + dz) % 16, me["x"])
            self.copy(2, self.w_z.at[me["z"]], self.w_z.at[me["z"]], to)

    def exchange_table(self):
        me = self.me
        low = me["z"] % 8
        for dz in (4, 3, 5, 2, 6, 1, 7):
            to = device(me["core"], me["y"], me["z"] - low + (low + dz) % 8, me["x"])
            self.copy(3, self.t_z.at[low], self.t_z.at[low], to)

    def exchanged(self):
        self.wait(2)
        total = self.w_z[0].astype(f32)
        for slot in range(1, 16):
            total = total + self.w_z[slot].astype(f32)
        self.w_all[self.w_at] = total.astype(bf16)

    def exchanged_table(self):
        self.wait(3)
        total = self.t_z[0].astype(f32)
        for slot in range(1, 8):
            total = total + self.t_z[slot].astype(f32)
        self.t_all[piece(self.t_at, 32)] = total.astype(bf16)

    def gather(self):
        for offset in PLANE:
            self.copy(4, self.w_all.at[self.w_at], self.w_all.at[self.w_at], self.plane(*offset)[2])

    def gather_table(self):
        own = piece(self.t_at, 32)
        for offset in YC:
            self.copy(5, self.t_all.at[own], self.t_all.at[own], self.plane(0, *offset)[2])

    def gathered(self, w_ref, t_ref):
        self.wait(4)
        w_ref[...] = self.w_all[...]
        self.wait(5)
        t_ref[...] = self.t_all[...]


def finish(scale, table_scale, grid_a, grid_b, w_one, w_two, t_one, t_two,
           out_ref, field_ref, gains_ref, qkv_ref, proj_ref, table_ref, flat_ref):
    out_ref[...] = grid_a[...]
    field_ref[...] = grid_b[...]
    for block, (w_all, t_all) in enumerate(((w_one, t_one), (w_two, t_two))):
        tiles = [w_all[4 * tile : 4 * tile + 4].astype(f32).reshape(ROWS, 128) * scale for tile in range(6)]
        for tile in range(4):
            qkv_ref[block, :, tile * 128 : (tile + 1) * 128] = tiles[tile]
        qkv_ref[block, :, 512:576] = tiles[4][:, :64]
        proj_ref[block] = jnp.concatenate([tiles[4][:, 64:], tiles[5]], axis=1)
        gains = w_all[24].astype(f32) * scale
        gains_ref[block : block + 1, :128] = gains[0:1]
        gains_ref[block : block + 1, 128:] = gains[1:2, :64]
        parts = [t_all[80 * tile : 80 * tile + 80].astype(f32) for tile in range(3)]
        table = jnp.concatenate(parts, axis=1) * table_scale
        for half, slot, starts in table_places(block):
            row = (half * 6 + slot) * 6
            for index, start in enumerate(starts):
                flat_ref[:, start : start + 138] = table[row : row + 6, index * 138 : index * 138 + 138]
        table_ref[block] = flat_ref[...].reshape(HEADS, 1, TAB)


def kernel(sizes, x_ref, ct_ref, gain_ref, w_qkv_ref, w_proj_ref, table_ref,
           out_ref, field_ref, w_one, w_two, t_one, t_two,
           flat_ref, lag_ref, bias_ref, p_ref, gs_ref, halo_src, halo_dst, halo_send, halo_recv, *sum_refs):
    n_lon, n_lat = sizes
    alone = n_lon * n_lat == 1
    me = place()
    if not alone:
        barrier = pltpu.get_barrier_semaphore()
        count = 0
        for dlat, dlon in ((0, 1), (1, 0), (1, 1)):
            for sign in (1, -1):
                to = {"lon": (me["lon"] + sign * dlon + n_lon) % n_lon, "lat": (me["lat"] + sign * dlat + n_lat) % n_lat}
                pl.semaphore_signal(barrier, inc=1, device_id=to, device_id_type=MESH)
                count += 1
        partners = [device((me["core"] + dc) % 2, (me["y"] + dy) % 4, me["z"], (me["x"] + dx) % 4) for dx, dy, dc in PLANE]
        partners += [device(me["core"], me["y"], (me["z"] + dz) % 16, me["x"]) for dz in FAR]
        for to in partners:
            pl.semaphore_signal(barrier, inc=1, device_id=to, device_id_type=MESH)
        count += len(partners)
    halos = [
        Halo(halo_src.at[n], halo_dst.at[n], halo_send.at[n], halo_recv.at[n], -1 if n < 2 else 1, sizes)
        for n in range(4)
    ]
    first, turned, second, back = halos

    def exchange(halo, rows):
        halo.src[...] = rows
        if alone:
            for half in range(2):
                for lon_half in range(2):
                    start = half * 96 + lon_half * QUAD
                    end = (1 - half) * 96 + (1 - lon_half) * QUAD
                    halo.dst[end : end + QUAD] = halo.src[start : start + QUAD]
        else:
            halo.start()

    def arrived(halo):
        if not alone:
            halo.finish()
        return halo.dst[...]

    last = me["lat"] == n_lat - 1
    to_rows = to_rows_matrix()
    from_rows = from_rows_matrix()
    x_rows = mm(to_rows, load_grid(x_ref))
    ct_rows = mm(to_rows, load_grid(ct_ref)).astype(bf16)
    build_lags(lag_ref)
    expand(table_ref, flat_ref, lag_ref, bias_ref, 0, last)
    gain = [gain_ref[0:1], gain_ref[1:2]]
    w_qkv = [w_qkv_ref[0], w_qkv_ref[1]]
    w_proj = [w_proj_ref[0], w_proj_ref[1]]
    first_out, saved_first = forward(0, x_rows, gain[0], w_qkv[0], w_proj[0], bias_ref, p_ref)
    if not alone:
        pl.semaphore_wait(barrier, count)
    exchange(first, first_out.astype(bf16))
    exchange(turned, ct_rows)
    expand(table_ref, flat_ref, lag_ref, bias_ref, 1, last)
    shifted = arrived(first).astype(f32)
    second_out, saved_second = forward(1, shifted, gain[1], w_qkv[1], w_proj[1], bias_ref, p_ref)
    exchange(second, second_out.astype(bf16))
    grad_second = arrived(turned)
    grad_shifted, gain_two, sums_two = backward(1, saved_second, grad_second, gain[1], w_qkv[1], w_proj[1], p_ref, gs_ref)
    exchange(back, grad_shifted)
    half = len(sum_refs) // 2
    two = Sums(sum_refs[: half - 2], *sum_refs[half - 2 : half])
    one = Sums(sum_refs[half : 2 * half - 2], *sum_refs[2 * half - 2 :])
    two.fill(sums_two, gain_two)
    if not alone:
        two.scatter()
    two.fill_table(reduce_lags(gs_ref, lag_ref))
    if not alone:
        two.scatter_table()
    grad_first = arrived(back)
    grad_field, gain_one, sums_one = backward(0, saved_first, grad_first, gain[0], w_qkv[0], w_proj[0], p_ref, gs_ref)
    one.fill(sums_one, gain_one)
    if alone:
        one.fill_table(reduce_lags(gs_ref, lag_ref))
        for sums, w_ref, t_ref in ((one, w_one, t_one), (two, w_two, t_two)):
            w_ref[...] = sums.w_src[...]
            t_ref[...] = sums.t_src[...]
    else:
        one.scatter()
        two.scattered()
        two.exchange()
        two.scattered_table()
        two.exchange_table()
        one.fill_table(reduce_lags(gs_ref, lag_ref))
        one.scatter_table()
    store_grid(field_ref, mm(from_rows, grad_field))
    store_grid(out_ref, mm(from_rows, arrived(second)))
    if not alone:
        one.scattered()
        one.exchange()
        one.scattered_table()
        one.exchange_table()
        two.exchanged()
        two.gather()
        two.exchanged_table()
        two.gather_table()
        for halo in halos:
            halo.drain()
        one.exchanged()
        one.gather()
        one.exchanged_table()
        one.gather_table()
        two.gathered(w_two, t_two)
        two.drain()
        one.gathered(w_one, t_one)
        one.drain()


def per_device(fields, cotangent, norm_gains, w_qkv, w_proj, tables, *, sizes, interpret=False):
    n_lon, n_lat = sizes
    scale = float(2 * 6 * n_lat * 12 * n_lon) ** -0.5
    table_scale = float(n_lon) ** -0.5
    vmem = pl.BlockSpec(memory_space=pltpu.VMEM)
    grid = jax.ShapeDtypeStruct((6, 12, 2, C), bf16)
    w_shape, t_shape = (32, 48, 128), (256, 128)
    many = n_lon * n_lat > 1
    sum_scratch = [
        pltpu.VMEM(w_shape, bf16),
        pltpu.VMEM(t_shape, bf16),
        pltpu.VMEM((31, 48, 128), bf16),
        pltpu.VMEM((7, 32, 128), bf16),
        pltpu.VMEM((16, 48, 128), bf16),
        pltpu.VMEM((8, 32, 128), bf16),
        pltpu.VMEM(w_shape, bf16),
        pltpu.VMEM(t_shape, bf16),
        pltpu.SemaphoreType.DMA((6,)),
        pltpu.SemaphoreType.DMA((6,)),
    ]
    found = pl.pallas_call(
        functools.partial(kernel, sizes),
        out_shape=[grid, grid] + [jax.ShapeDtypeStruct(w_shape, bf16)] * 2 + [jax.ShapeDtypeStruct(t_shape, bf16)] * 2,
        in_specs=[vmem] * 6,
        out_specs=[vmem] * 6,
        scratch_shapes=[
            pltpu.VMEM((HEADS, 2, 8, LAGS), f32),
            pltpu.VMEM((12, ROWS, LAGS), bf16),
            pltpu.VMEM((2, HEADS, 2, 12, 8, ROWS), f32),
            pltpu.VMEM((2, HEADS, ROWS, ROWS), f32),
            pltpu.VMEM((HEADS, 2, 12, 8, ROWS), f32),
            pltpu.VMEM((4, ROWS, C), bf16),
            pltpu.VMEM((4, ROWS, C), bf16),
            pltpu.SemaphoreType.DMA((4, 3)),
            pltpu.SemaphoreType.DMA((4, 3)),
        ]
        + sum_scratch * 2,
        compiler_params=pltpu.CompilerParams(
            collective_id=0 if many else None, has_side_effects=True, vmem_limit_bytes=56 * 2**20
        ),
        interpret=interpret,
    )(
        fields.transpose(1, 2, 0, 3),
        cotangent.transpose(1, 2, 0, 3),
        norm_gains,
        w_qkv,
        w_proj,
        tables.transpose(0, 2, 1, 3),
    )
    outs = pl.pallas_call(
        functools.partial(finish, scale, table_scale),
        out_shape=[
            grid,
            grid,
            jax.ShapeDtypeStruct((2, C), f32),
            jax.ShapeDtypeStruct((2, C, 3 * C), f32),
            jax.ShapeDtypeStruct((2, C, C), f32),
            jax.ShapeDtypeStruct((2, HEADS, 1, TAB), f32),
        ],
        in_specs=[vmem] * 6,
        out_specs=[vmem] * 6,
        scratch_shapes=[pltpu.VMEM((HEADS, TAB), f32)],
        compiler_params=pltpu.CompilerParams(vmem_limit_bytes=32 * 2**20),
        interpret=interpret,
    )(*found)
    grids = [rows.transpose(2, 0, 1, 3) for rows in outs[:2]]
    return (*grids, *outs[2:5], outs[5].transpose(0, 2, 1, 3))


def solution(mesh):
    grid = P(None, "lat", "lon", None)
    bands = P(None, "lat", None, None)
    sizes = (mesh.shape["lon"], mesh.shape["lat"])
    return jax.shard_map(
        functools.partial(per_device, sizes=sizes),
        mesh=mesh,
        in_specs=(grid, grid, P(), P(), P(), bands),
        out_specs=(grid, grid, P(), P(), P(), bands),
        check_vma=False,
    )
```

time: 101 us -> 85.2 us (0.84)
  local copies, waits for them, and re-layouts: 15.7 us -> 5.43 us
  Pallas kernels: 84.2 us -> 78.7 us
    pallas_call x1 -> x2, Pallas kernels: 84.2 us -> 78.7 us  [the longest x1 77.2 us: per_device(): pl.pallas_call(functools.partial(kernel, sizes), out_shape=[grid, grid] +...]
    unnamed x17 -> x12, local copies, waits for them, and re-layouts: 10.2 us -> 5.43 us
    reshape x3 -> x0, local copies, waits for them, and re-layouts: 2.36 us -> none  [the longest x1 0.98 us: restore(): shaped = lagged[:, :, :LAGS].reshape(2, HEADS * 2, 8, LAGS)[:, :, :6]]
    slice x4 -> x0, local copies, waits for them, and re-layouts: 1.86 us -> none  [the longest x2 1.67 us: arrange(): shaped = jnp.stack([shaped[0], shaped[1][:, ::-1, ::-1]])]
where the time goes in v2:
time: 85.2 us; the launch traced here: 84.8 us
  Pallas kernels  78.7 us (92%)
  local copies, waits for them, and re-layouts  5.43 us (6%)
    pallas_call x1, Pallas kernels, per_device(): pl.pallas_call(functools.partial(kernel, sizes), out_shape=[grid, grid] +...  77.2 us
    unnamed x12, local copies, waits for them, and re-layouts  5.43 us

profile of v2, /device:TPU:1, one launch (start us, length us, event | category | flops | bytes accessed | tf_op | source)
XLA Modules:
  0.0 84.8 jit_solution(891626845468499745)
XLA Ops:
  0.6 77.2 %shard_map.109 = (bf16[6,12,2,192]{3,2,1,0:T(2,128)(2,1)}, bf16[6,12,2,192]{3,2,1,0:T(2,128)(2,1)}, bf16[32,48,128]{2,1,0:T(8,128)(2,1)}, bf16[32,48,128]{2,1,0:...) custom-call(bf16[6,12,2,192]{3,2,1,0:T(2,128)(2,1)} %bitcast.7, bf16[6,12,2,192]{3,2,1,0:T(2,128)(2,1)} %bitcast.8, ...), custom_call_target="tpu_custom_call" | custom-call | tf_op jit(solution)/shard_map/pallas_call | solution.py:534
  77.8 0.0 copy-start
  77.9 1.0 %copy-done = bf16[32,48,128]{2,1,0:T(8,128)(2,1)S(1)} copy-done((bf16[32,48,128]{2,1,0:T(8,128)(2,1)S(1)}, bf16[32,48,128]{2,1,0:T(8,128)(2,1)}, u32[]{:S(2)}) %copy-start) | copy-done | bytes 393240
  78.8 0.0 copy-start.1
  78.8 1.0 %copy-done.1 = bf16[32,48,128]{2,1,0:T(8,128)(2,1)S(1)} copy-done((bf16[32,48,128]{2,1,0:T(8,128)(2,1)S(1)}, bf16[32,48,128]{2,1,0:T(8,128)(2,1)}, u32[]{:S(2)}) %copy-start.1) | copy-done | bytes 393240
  79.8 0.0 copy-start.2
  79.8 0.9 %copy-done.2 = bf16[6,12,2,192]{3,2,1,0:T(2,128)(2,1)S(1)} copy-done((bf16[6,12,2,192]{3,2,1,0:T(2,128)(2,1)S(1)}, bf16[6,12,2,192]{3,2,1,0:T(2,128)(2,1)}, u32[]{:S(2)}) %copy-start.2) | copy-done | bytes 55320
  80.7 0.0 copy-start.3
  80.7 0.9 %copy-done.3 = bf16[6,12,2,192]{3,2,1,0:T(2,128)(2,1)S(1)} copy-done((bf16[6,12,2,192]{3,2,1,0:T(2,128)(2,1)S(1)}, bf16[6,12,2,192]{3,2,1,0:T(2,128)(2,1)}, u32[]{:S(2)}) %copy-start.3) | copy-done | bytes 55320
  81.6 0.0 copy-start.4
  81.6 0.8 copy-done.4
  82.4 0.0 copy-start.5
  82.4 0.8 copy-done.5
  83.3 1.5 %shard_map.110 = (bf16[6,12,2,192]{3,2,1,0:T(2,128)(2,1)}, bf16[6,12,2,192]{3,2,1,0:T(2,128)(2,1)}, f32[2,192]{1,0:T(2,128)}, f32[2,192,576]{2,1,0:T(8,128)}, f3...) custom-call(bf16[6,12,2,192]{3,2,1,0:T(2,128)(2,1)S(1)} %copy-done.2, bf16[6,12,2,192]{3,2,1,0:T(2,128)(2,1)S(1)} %copy-done.3, ...), custom_call_target="tpu_custom_call" | custom-call | tf_op jit(solution)/shard_map/pallas_call | solution.py:563
Async XLA Ops:
  77.8 1.0 %copy-start = (bf16[32,48,128]{2,1,0:T(8,128)(2,1)S(1)}, bf16[32,48,128]{2,1,0:T(8,128)(2,1)}, u32[]{:S(2)}) copy-start(bf16[32,48,128]{2,1,0:T(8,128)(2,1)} %get-tuple-element.20.w_one) | copy-start | bytes 1179652
  78.8 1.0 %copy-start.1 = (bf16[32,48,128]{2,1,0:T(8,128)(2,1)S(1)}, bf16[32,48,128]{2,1,0:T(8,128)(2,1)}, u32[]{:S(2)}) copy-start(bf16[32,48,128]{2,1,0:T(8,128)(2,1)} %get-tuple-element.21.w_two) | copy-start | bytes 1179652
  79.8 0.9 %copy-start.2 = (bf16[6,12,2,192]{3,2,1,0:T(2,128)(2,1)S(1)}, bf16[6,12,2,192]{3,2,1,0:T(2,128)(2,1)}, u32[]{:S(2)}) copy-start(bf16[6,12,2,192]{3,2,1,0:T(2,128)(2,1)} %get-tuple-element.18.grid_a) | copy-start | bytes 165892
  80.7 0.9 %copy-start.3 = (bf16[6,12,2,192]{3,2,1,0:T(2,128)(2,1)S(1)}, bf16[6,12,2,192]{3,2,1,0:T(2,128)(2,1)}, u32[]{:S(2)}) copy-start(bf16[6,12,2,192]{3,2,1,0:T(2,128)(2,1)} %get-tuple-element.19.grid_b) | copy-start | bytes 165892
  81.6 0.8 copy-start.4
  82.4 0.8 copy-start.5

commit v3 on v2

--- a/solution.py
+++ b/solution.py
@@ -161,7 +161,6 @@
 
 def backward(block, saved, grad_b, gain, w_qkv, w_proj, p_ref, gs_ref):
     normed, inv_std, normed_b, q, k, v, mixed_b = saved
-    proj_sum = mm_tn(mixed_b, grad_b)
     grad_mixed = mm_nt(grad_b, w_proj).astype(bf16)
     grad_q = jnp.zeros((ROWS, C), f32)
     grad_k = jnp.zeros((ROWS, C), f32)
@@ -181,7 +180,7 @@
     grad_k = (grad_k * SCALE).astype(bf16)
     grad_v = grad_v.astype(bf16)
     sums = jnp.concatenate(
-        [mm_tn(normed_b, grad_q), mm_tn(normed_b, grad_k), mm_tn(normed_b, grad_v), proj_sum], axis=1
+        [mm_tn(normed_b, grad_q), mm_tn(normed_b, grad_k), mm_tn(normed_b, grad_v)], axis=1
     )
     grad_normed = mm_nt(grad_q, w_qkv[:, :C]) + mm_nt(grad_k, w_qkv[:, C : 2 * C])
     grad_normed = grad_normed + mm_nt(grad_v, w_qkv[:, 2 * C :])
@@ -195,14 +194,12 @@
 
 def place():
     lon, lat = lax.axis_index("lon"), lax.axis_index("lat")
-    return dict(core=lon % 2, y=(lon // 2) % 4, z=(lat // 4) * 8 + lon // 8, x=lat % 4, lon=lon, lat=lat)
-
-
-def device(core, y, z, x):
-    return {"lon": ((z % 8) * 4 + y) * 2 + core, "lat": (z // 8) * 4 + x}
-
-
-XY = [(dx, dy) for dx in range(4) for dy in range(4) if (dx, dy) != (0, 0)]
+    core, y, low = lax.rem(lon, 2), lax.rem(lax.div(lon, 2), 4), lax.div(lon, 8)
+    return dict(core=core, y=y, low=low, high=lax.div(lat, 4), x=lax.rem(lat, 4), lon=lon, lat=lat)
+
+
+def device(core, y, low, high, x):
+    return {"lon": (low * 4 + y) * 2 + core, "lat": high * 4 + x}
 
 
 class Halo:
@@ -216,12 +213,12 @@
         found = []
         for slot, (half, lon_half) in enumerate([(0, 0), (0, 1), (1, 0)]):
             if self.towards < 0:
-                lat = (me["lat"] - (1 - half) + n_lat) % n_lat
-                lon = (me["lon"] - (1 - lon_half) + n_lon) % n_lon
+                lat = lax.rem(me["lat"] - (1 - half) + n_lat, n_lat)
+                lon = lax.rem(me["lon"] - (1 - lon_half) + n_lon, n_lon)
                 source = (half, lon_half)
             else:
-                lat = (me["lat"] + half_of(half)) % n_lat
-                lon = (me["lon"] + half_of(lon_half)) % n_lon
+                lat = lax.rem(me["lat"] + 1 - half, n_lat)
+                lon = lax.rem(me["lon"] + 1 - lon_half, n_lon)
                 source = (1 - half, 1 - lon_half)
             start = source[0] * 96 + source[1] * QUAD
             end = (1 - source[0]) * 96 + (1 - source[1]) * QUAD
@@ -253,26 +250,29 @@
             copy.wait_send()
 
 
-def half_of(half):
-    return 1 - half
-
-
-PLANE = [(dx, dy, dc) for dx in (2, 1, 3, 0) for dy in (2, 1, 3, 0) for dc in (1, 0) if (dx, dy, dc) != (0, 0, 0)]
-YC = [(dy, dc) for dy in (2, 1, 3, 0) for dc in (1, 0) if (dy, dc) != (0, 0)]
-FAR = (8, 7, 9, 6, 10, 5, 11, 4, 12, 3, 13, 2, 14, 1, 15)
+NEAR = [(0, dy, dc) for dy in (2, 1, 3, 0) for dc in (1, 0) if (dy, dc) != (0, 0)]
+WIDE = [(dx, dy, dc) for dx in (2, 1, 3) for dy in (2, 1, 3, 0) for dc in (1, 0)]
+T_ROWS = 32
 
 
 def piece(index, rows):
     return pl.ds(pl.multiple_of(index * rows, rows), rows)
 
 
+def weight_lanes(parts, gains):
+    rest = [gains[:, 64 * n : 64 * n + 64] for n in range(3)] + [jnp.zeros((ROWS - 3, 64), f32)]
+    return jnp.concatenate(parts + [jnp.concatenate(rest, axis=0)], axis=1)
+
+
 class Sums:
     def __init__(self, refs, send, recv):
-        self.w_src, self.t_src, self.w_in, self.t_in, self.w_z, self.t_z, self.w_all, self.t_all = refs
+        self.w_src, self.t_src, self.w_in, self.t_in, self.along, self.all = refs
+        self.rows = self.w_src.shape[1]
         self.send, self.recv = send, recv
         self.me = me = place()
-        self.w_at = (me["y"] * 4 + me["x"]) * 2 + me["core"]
+        self.at = (me["y"] * 4 + me["x"]) * 2 + me["core"]
         self.t_at = me["y"] * 2 + me["core"]
+        self.z_at = me["high"] * 8 + me["low"]
 
     def copy(self, step, src, dst, to):
         pltpu.make_async_remote_copy(
@@ -281,7 +281,8 @@
         ).start()
 
     def total(self, step):
-        return (self.w_in, self.t_in, self.w_z.at[pl.ds(0, 15)], self.t_z.at[pl.ds(0, 7)], self.w_in, self.t_in)[step]
+        near = self.all.at[pl.ds(0, len(NEAR))]
+        return (self.w_in, self.t_in, near, self.w_in.at[pl.ds(0, 8)], near, self.w_in.at[pl.ds(0, len(WIDE))])[step]
 
     def wait(self, step):
         pltpu.make_async_copy(self.total(step), self.total(step), self.recv.at[step]).wait()
@@ -290,14 +291,13 @@
         for step in range(6):
             pltpu.make_async_copy(self.total(step), self.total(step), self.send.at[step]).wait()
 
-    def fill(self, sums, gains):
-        for tile in range(6):
-            lanes = sums[:, tile * 128 : (tile + 1) * 128]
-            self.w_src[4 * tile : 4 * tile + 4] = lanes.reshape(4, 48, 128).astype(bf16)
-        self.w_src[24:32] = jnp.zeros((8, 48, 128), bf16)
-        gains = jnp.concatenate([gains, jnp.zeros((1, 64), f32)], axis=1)
-        gains = jnp.concatenate([gains[:, :128], gains[:, 128:], jnp.zeros((46, 128), f32)], axis=0)
-        self.w_src[24] = gains.astype(bf16)
+    def fill(self, lanes):
+        each, tiles = ROWS // self.rows, lanes.shape[1] // 128
+        for tile in range(tiles):
+            part = lanes[:, tile * 128 : (tile + 1) * 128]
+            self.w_src[each * tile : each * tile + each] = part.reshape(each, self.rows, 128).astype(bf16)
+        if each * tiles < 32:
+            self.w_src[each * tiles :] = jnp.zeros((32 - each * tiles, self.rows, 128), bf16)
 
     def fill_table(self, table):
         table = jnp.concatenate([table, jnp.zeros((96, 384 - LAGS), f32)], axis=1)
@@ -308,89 +308,95 @@
 
     def plane(self, dx, dy, dc):
         me = self.me
-        x, y, core = (me["x"] + dx) % 4, (me["y"] + dy) % 4, (me["core"] + dc) % 2
-        return (y * 4 + x) * 2 + core, y * 2 + core, device(core, y, me["z"], x)
+        x, y, core = lax.rem(me["x"] + dx, 4), lax.rem(me["y"] + dy, 4), lax.rem(me["core"] + dc, 2)
+        return (y * 4 + x) * 2 + core, y * 2 + core, device(core, y, me["low"], me["high"], x)
 
     def scatter(self):
-        for slot, offset in enumerate(PLANE):
+        for slot, offset in enumerate(WIDE + NEAR):
             at, _, to = self.plane(*offset)
             self.copy(0, self.w_src.at[at], self.w_in.at[slot], to)
 
     def scatter_table(self):
-        for slot, offset in enumerate(YC):
-            _, at, to = self.plane(0, *offset)
-            self.copy(1, self.t_src.at[piece(at, 32)], self.t_in.at[slot], to)
+        for slot, offset in enumerate(NEAR):
+            _, at, to = self.plane(*offset)
+            self.copy(1, self.t_src.at[piece(at, T_ROWS)], self.t_in.at[slot], to)
 
     def scattered(self):
         self.wait(0)
-        total = self.w_src[self.w_at].astype(f32)
+        total = self.w_src[self.at].astype(f32)
         for slot in range(31):
             total = total + self.w_in[slot].astype(f32)
-        self.w_z[self.me["z"]] = total.astype(bf16)
+        self.along[self.z_at, : self.rows] = total.astype(bf16)
 
     def scattered_table(self):
         self.wait(1)
-        total = self.t_src[piece(self.t_at, 32)].astype(f32)
-        for slot in range(7):
+        total = self.t_src[piece(self.t_at, T_ROWS)].astype(f32)
+        for slot in range(len(NEAR)):
             total = total + self.t_in[slot].astype(f32)
-        self.t_z[self.me["z"] % 8] = total.astype(bf16)
+        self.along[self.z_at, self.rows :] = total.astype(bf16)
+
+    def line(self, dz, other):
+        me = self.me
+        high = 1 - me["high"] if other else me["high"]
+        return device(me["core"], me["y"], lax.rem(me["low"] + dz, 8), high, me["x"])
 
     def exchange(self):
-        me = self.me
-        for dz in FAR:
-            to = device(me["core"], me["y"], (me["z"] + dz) % 16, me["x"])
-            self.copy(2, self.w_z.at[me["z"]], self.w_z.at[me["z"]], to)
-
-    def exchange_table(self):
-        me = self.me
-        low = me["z"] % 8
+        own = self.along.at[self.z_at, pl.ds(0, self.rows)]
+        for dz in (0, 1, 7, 2, 6, 3, 5, 4):
+            self.copy(3, own, own, self.line(dz, True))
+
+    def exchange_near(self):
+        own = self.along.at[self.z_at]
         for dz in (4, 3, 5, 2, 6, 1, 7):
-            to = device(me["core"], me["y"], me["z"] - low + (low + dz) % 8, me["x"])
-            self.copy(3, self.t_z.at[low], self.t_z.at[low], to)
+            self.copy(2, own, own, self.line(dz, False))
 
     def exchanged(self):
         self.wait(2)
-        total = self.w_z[0].astype(f32)
+        self.wait(3)
+        weights = self.along[0, : self.rows].astype(f32)
         for slot in range(1, 16):
-            total = total + self.w_z[slot].astype(f32)
-        self.w_all[self.w_at] = total.astype(bf16)
-
-    def exchanged_table(self):
-        self.wait(3)
-        total = self.t_z[0].astype(f32)
+            weights = weights + self.along[slot, : self.rows].astype(f32)
+        self.all[self.at, : self.rows] = weights.astype(bf16)
+        base = self.me["high"] * 8
+        table = self.along[base, self.rows :].astype(f32)
         for slot in range(1, 8):
-            total = total + self.t_z[slot].astype(f32)
-        self.t_all[piece(self.t_at, 32)] = total.astype(bf16)
+            table = table + self.along[base + slot, self.rows :].astype(f32)
+        self.all[self.at, self.rows :] = table.astype(bf16)
 
     def gather(self):
-        for offset in PLANE:
-            self.copy(4, self.w_all.at[self.w_at], self.w_all.at[self.w_at], self.plane(*offset)[2])
-
-    def gather_table(self):
-        own = piece(self.t_at, 32)
-        for offset in YC:
-            self.copy(5, self.t_all.at[own], self.t_all.at[own], self.plane(0, *offset)[2])
+        own = self.all.at[self.at, pl.ds(0, self.rows)]
+        for offset in WIDE:
+            self.copy(5, own, own, self.plane(*offset)[2])
+        own = self.all.at[self.at]
+        for offset in NEAR:
+            self.copy(4, own, own, self.plane(*offset)[2])
 
     def gathered(self, w_ref, t_ref):
         self.wait(4)
-        w_ref[...] = self.w_all[...]
         self.wait(5)
-        t_ref[...] = self.t_all[...]
+        w_ref[...] = self.all[:, : self.rows]
+        for y in range(4):
+            for core in range(2):
+                at = y * 2 + core
+                t_ref[at * T_ROWS : at * T_ROWS + T_ROWS] = self.all[(y * 4 + self.me["x"]) * 2 + core, self.rows :]
 
 
 def finish(scale, table_scale, grid_a, grid_b, w_one, w_two, t_one, t_two,
            out_ref, field_ref, gains_ref, qkv_ref, proj_ref, table_ref, flat_ref):
     out_ref[...] = grid_a[...]
     field_ref[...] = grid_b[...]
-    for block, (w_all, t_all) in enumerate(((w_one, t_one), (w_two, t_two))):
-        tiles = [w_all[4 * tile : 4 * tile + 4].astype(f32).reshape(ROWS, 128) * scale for tile in range(6)]
+    for block, (w_all, t_all, rows, count) in enumerate(((w_one, t_one, 32, 5), (w_two, t_two, 48, 8))):
+        each = ROWS // rows
+        tiles = [w_all[each * n : each * n + each].astype(f32).reshape(ROWS, 128) * scale for n in range(count)]
         for tile in range(4):
             qkv_ref[block, :, tile * 128 : (tile + 1) * 128] = tiles[tile]
         qkv_ref[block, :, 512:576] = tiles[4][:, :64]
-        proj_ref[block] = jnp.concatenate([tiles[4][:, 64:], tiles[5]], axis=1)
-        gains = w_all[24].astype(f32) * scale
-        gains_ref[block : block + 1, :128] = gains[0:1]
-        gains_ref[block : block + 1, 128:] = gains[1:2, :64]
+        if block:
+            proj_ref[1] = jnp.concatenate([tiles[4][:, 64:], tiles[5]], axis=1)
+            proj_ref[0, :, :128] = tiles[6]
+            proj_ref[0, :, 128:] = tiles[7][:, :64]
+        gains = tiles[-1][:8, 64:]
+        gains_ref[block : block + 1] = jnp.concatenate([gains[n : n + 1] for n in range(3)], axis=1)
         parts = [t_all[80 * tile : 80 * tile + 80].astype(f32) for tile in range(3)]
         table = jnp.concatenate(parts, axis=1) * table_scale
         for half, slot, starts in table_places(block):
@@ -411,19 +417,25 @@
         count = 0
         for dlat, dlon in ((0, 1), (1, 0), (1, 1)):
             for sign in (1, -1):
-                to = {"lon": (me["lon"] + sign * dlon + n_lon) % n_lon, "lat": (me["lat"] + sign * dlat + n_lat) % n_lat}
+                to = {"lon": lax.rem(me["lon"] + sign * dlon + n_lon, n_lon), "lat": lax.rem(me["lat"] + sign * dlat + n_lat, n_lat)}
                 pl.semaphore_signal(barrier, inc=1, device_id=to, device_id_type=MESH)
                 count += 1
-        partners = [device((me["core"] + dc) % 2, (me["y"] + dy) % 4, me["z"], (me["x"] + dx) % 4) for dx, dy, dc in PLANE]
-        partners += [device(me["core"], me["y"], (me["z"] + dz) % 16, me["x"]) for dz in FAR]
+        partners = []
+        for dx, dy, dc in WIDE + NEAR:
+            x, y, core = lax.rem(me["x"] + dx, 4), lax.rem(me["y"] + dy, 4), lax.rem(me["core"] + dc, 2)
+            partners.append(device(core, y, me["low"], me["high"], x))
+        for dz in range(8):
+            partners.append(device(me["core"], me["y"], lax.rem(me["low"] + dz, 8), 1 - me["high"], me["x"]))
+            if dz:
+                partners.append(device(me["core"], me["y"], lax.rem(me["low"] + dz, 8), me["high"], me["x"]))
         for to in partners:
             pl.semaphore_signal(barrier, inc=1, device_id=to, device_id_type=MESH)
         count += len(partners)
     halos = [
-        Halo(halo_src.at[n], halo_dst.at[n], halo_send.at[n], halo_recv.at[n], -1 if n < 2 else 1, sizes)
-        for n in range(4)
+        Halo(halo_src.at[n], halo_dst.at[n], halo_send.at[n], halo_recv.at[n], 1 if n in (2, 3) else -1, sizes)
+        for n in range(5)
     ]
-    first, turned, second, back = halos
+    first, turned, second, back, shared = halos
 
     def exchange(halo, rows):
         halo.src[...] = rows
@@ -456,6 +468,7 @@
         pl.semaphore_wait(barrier, count)
     exchange(first, first_out.astype(bf16))
     exchange(turned, ct_rows)
+    exchange(shared, saved_first[-1])
     expand(table_ref, flat_ref, lag_ref, bias_ref, 1, last)
     shifted = arrived(first).astype(f32)
     second_out, saved_second = forward(1, shifted, gain[1], w_qkv[1], w_proj[1], bias_ref, p_ref)
@@ -466,7 +479,9 @@
     half = len(sum_refs) // 2
     two = Sums(sum_refs[: half - 2], *sum_refs[half - 2 : half])
     one = Sums(sum_refs[half : 2 * half - 2], *sum_refs[2 * half - 2 :])
-    two.fill(sums_two, gain_two)
+    proj_one = mm_tn(arrived(shared), grad_shifted)
+    proj_two = mm_tn(saved_second[-1], grad_second)
+    two.fill(weight_lanes([sums_two, proj_two, proj_one], gain_two))
     if not alone:
         two.scatter()
     two.fill_table(reduce_lags(gs_ref, lag_ref))
@@ -474,7 +489,7 @@
         two.scatter_table()
     grad_first = arrived(back)
     grad_field, gain_one, sums_one = backward(0, saved_first, grad_first, gain[0], w_qkv[0], w_proj[0], p_ref, gs_ref)
-    one.fill(sums_one, gain_one)
+    one.fill(weight_lanes([sums_one], gain_one))
     if alone:
         one.fill_table(reduce_lags(gs_ref, lag_ref))
         for sums, w_ref, t_ref in ((one, w_one, t_one), (two, w_two, t_two)):
@@ -485,7 +500,7 @@
         two.scattered()
         two.exchange()
         two.scattered_table()
-        two.exchange_table()
+        two.exchange_near()
         one.fill_table(reduce_lags(gs_ref, lag_ref))
         one.scatter_table()
     store_grid(field_ref, mm(from_rows, grad_field))
@@ -494,17 +509,13 @@
         one.scattered()
         one.exchange()
         one.scattered_table()
-        one.exchange_table()
+        one.exchange_near()
         two.exchanged()
         two.gather()
-        two.exchanged_table()
-        two.gather_table()
         for halo in halos:
             halo.drain()
         one.exchanged()
         one.gather()
-        one.exchanged_table()
-        one.gather_table()
         two.gathered(w_two, t_two)
         two.drain()
         one.gathered(w_one, t_one)
@@ -517,23 +528,25 @@
     table_scale = float(n_lon) ** -0.5
     vmem = pl.BlockSpec(memory_space=pltpu.VMEM)
     grid = jax.ShapeDtypeStruct((6, 12, 2, C), bf16)
-    w_shape, t_shape = (32, 48, 128), (256, 128)
+    w_one, w_two, t_shape = (32, 32, 128), (32, 48, 128), (256, 128)
     many = n_lon * n_lat > 1
-    sum_scratch = [
-        pltpu.VMEM(w_shape, bf16),
-        pltpu.VMEM(t_shape, bf16),
-        pltpu.VMEM((31, 48, 128), bf16),
-        pltpu.VMEM((7, 32, 128), bf16),
-        pltpu.VMEM((16, 48, 128), bf16),
-        pltpu.VMEM((8, 32, 128), bf16),
-        pltpu.VMEM(w_shape, bf16),
-        pltpu.VMEM(t_shape, bf16),
-        pltpu.SemaphoreType.DMA((6,)),
-        pltpu.SemaphoreType.DMA((6,)),
-    ]
+
+    def scratch(w_shape):
+        part = w_shape[1] + T_ROWS
+        return [
+            pltpu.VMEM(w_shape, bf16),
+            pltpu.VMEM(t_shape, bf16),
+            pltpu.VMEM((31, w_shape[1], 128), bf16),
+            pltpu.VMEM((len(NEAR), T_ROWS, 128), bf16),
+            pltpu.VMEM((16, part, 128), bf16),
+            pltpu.VMEM((32, part, 128), bf16),
+            pltpu.SemaphoreType.DMA((6,)),
+            pltpu.SemaphoreType.DMA((6,)),
+        ]
+
     found = pl.pallas_call(
         functools.partial(kernel, sizes),
-        out_shape=[grid, grid] + [jax.ShapeDtypeStruct(w_shape, bf16)] * 2 + [jax.ShapeDtypeStruct(t_shape, bf16)] * 2,
+        out_shape=[grid, grid] + [jax.ShapeDtypeStruct(shape, bf16) for shape in (w_one, w_two, t_shape, t_shape)],
         in_specs=[vmem] * 6,
         out_specs=[vmem] * 6,
         scratch_shapes=[
@@ -542,12 +555,13 @@
             pltpu.VMEM((2, HEADS, 2, 12, 8, ROWS), f32),
             pltpu.VMEM((2, HEADS, ROWS, ROWS), f32),
             pltpu.VMEM((HEADS, 2, 12, 8, ROWS), f32),
-            pltpu.VMEM((4, ROWS, C), bf16),
-            pltpu.VMEM((4, ROWS, C), bf16),
-            pltpu.SemaphoreType.DMA((4, 3)),
-            pltpu.SemaphoreType.DMA((4, 3)),
+            pltpu.VMEM((5, ROWS, C), bf16),
+            pltpu.VMEM((5, ROWS, C), bf16),
+            pltpu.SemaphoreType.DMA((5, 3)),
+            pltpu.SemaphoreType.DMA((5, 3)),
         ]
-        + sum_scratch * 2,
+        + scratch(w_two)
+        + scratch(w_one),
         compiler_params=pltpu.CompilerParams(
             collective_id=0 if many else None, has_side_effects=True, vmem_limit_bytes=56 * 2**20
         ),
@@ -573,7 +587,7 @@
         in_specs=[vmem] * 6,
         out_specs=[vmem] * 6,
         scratch_shapes=[pltpu.VMEM((HEADS, TAB), f32)],
-        compiler_params=pltpu.CompilerParams(vmem_limit_bytes=32 * 2**20),
+        compiler_params=pltpu.CompilerParams(vmem_limit_bytes=60 * 2**20),
         interpret=interpret,
     )(*found)
     grids = [rows.transpose(2, 0, 1, 3) for rows in outs[:2]]

time: 85.2 us -> 81.9 us (0.961)
  local copies, waits for them, and re-layouts: 5.43 us -> 0 us
  Pallas kernels: 78.7 us -> 81.1 us
    unnamed x12 -> x0, local copies, waits for them, and re-layouts: 5.43 us -> none
    pallas_call x1, Pallas kernels: 77.2 us -> 78.5 us  [per_device(): pl.pallas_call(functools.partial(kernel, sizes), out_shape=[grid, grid] +...]
    pallas_call x1, Pallas kernels: 1.48 us -> 2.6 us  [per_device(): pl.pallas_call(functools.partial(finish, scale, table_scale), out_shape=[...]
where the time goes in v3:
time: 81.9 us; the launch traced here: 81.7 us
  Pallas kernels  81.1 us (99%)
    pallas_call x1, Pallas kernels, per_device(): pl.pallas_call(functools.partial(kernel, sizes), out_shape=[grid, grid] +...  78.5 us
    pallas_call x1, Pallas kernels, per_device(): pl.pallas_call(functools.partial(finish, scale, table_scale), out_shape=[...  2.6 us

profile of v3, /device:TPU:1, one launch (start us, length us, event | category | flops | bytes accessed | tf_op | source)
XLA Modules:
  0.0 81.7 jit_solution(5330136799564379764)
XLA Ops:
  0.6 78.5 %shard_map.109 = (bf16[6,12,2,192]{3,2,1,0:T(2,128)(2,1)}, bf16[6,12,2,192]{3,2,1,0:T(2,128)(2,1)}, bf16[32,32,128]{2,1,0:T(8,128)(2,1)}, bf16[32,48,128]{2,1,0:...) custom-call(bf16[6,12,2,192]{3,2,1,0:T(2,128)(2,1)} %bitcast.7, bf16[6,12,2,192]{3,2,1,0:T(2,128)(2,1)} %bitcast.8, ...), custom_call_target="tpu_custom_call" | custom-call | tf_op jit(solution)/shard_map/pallas_call | solution.py:547
  79.1 2.6 %shard_map.110 = (bf16[6,12,2,192]{3,2,1,0:T(2,128)(2,1)}, bf16[6,12,2,192]{3,2,1,0:T(2,128)(2,1)}, f32[2,192]{1,0:T(2,128)}, f32[2,192,576]{2,1,0:T(8,128)}, f3...) custom-call(bf16[6,12,2,192]{3,2,1,0:T(2,128)(2,1)} %get-tuple-element.18.grid_a, ...), custom_call_target="tpu_custom_call" | custom-call | tf_op jit(solution)/shard_map/pallas_call | solution.py:577

commit v4 on v3

--- a/solution.py
+++ b/solution.py
@@ -179,17 +179,20 @@
     grad_q = (grad_q * SCALE).astype(bf16)
     grad_k = (grad_k * SCALE).astype(bf16)
     grad_v = grad_v.astype(bf16)
-    sums = jnp.concatenate(
-        [mm_tn(normed_b, grad_q), mm_tn(normed_b, grad_k), mm_tn(normed_b, grad_v)], axis=1
-    )
     grad_normed = mm_nt(grad_q, w_qkv[:, :C]) + mm_nt(grad_k, w_qkv[:, C : 2 * C])
     grad_normed = grad_normed + mm_nt(grad_v, w_qkv[:, 2 * C :])
     gain_sum = jnp.sum(grad_normed * normed, axis=0, keepdims=True)
-    grad_scaled = grad_normed * gain
-    grad_centre = grad_scaled - jnp.mean(grad_scaled, axis=-1, keepdims=True)
-    grad_centre = grad_centre - normed * jnp.mean(grad_scaled * normed, axis=-1, keepdims=True)
-    grad_in = (grad_b.astype(f32) + inv_std * grad_centre).astype(bf16)
-    return grad_in, gain_sum, sums
+
+    def weight_sums():
+        return jnp.concatenate([mm_tn(normed_b, part) for part in (grad_q, grad_k, grad_v)], axis=1)
+
+    def grad_in():
+        grad_scaled = grad_normed * gain
+        grad_centre = grad_scaled - jnp.mean(grad_scaled, axis=-1, keepdims=True)
+        grad_centre = grad_centre - normed * jnp.mean(grad_scaled * normed, axis=-1, keepdims=True)
+        return (grad_b.astype(f32) + inv_std * grad_centre).astype(bf16)
+
+    return grad_in, gain_sum, weight_sums
 
 
 def place():
@@ -474,8 +477,10 @@
     second_out, saved_second = forward(1, shifted, gain[1], w_qkv[1], w_proj[1], bias_ref, p_ref)
     exchange(second, second_out.astype(bf16))
     grad_second = arrived(turned)
-    grad_shifted, gain_two, sums_two = backward(1, saved_second, grad_second, gain[1], w_qkv[1], w_proj[1], p_ref, gs_ref)
+    grad_in, gain_two, weight_sums = backward(1, saved_second, grad_second, gain[1], w_qkv[1], w_proj[1], p_ref, gs_ref)
+    grad_shifted = grad_in()
     exchange(back, grad_shifted)
+    sums_two = weight_sums()
     half = len(sum_refs) // 2
     two = Sums(sum_refs[: half - 2], *sum_refs[half - 2 : half])
     one = Sums(sum_refs[half : 2 * half - 2], *sum_refs[2 * half - 2 :])
@@ -487,9 +492,13 @@
     two.fill_table(reduce_lags(gs_ref, lag_ref))
     if not alone:
         two.scatter_table()
+        two.scattered()
+        two.exchange()
+        two.scattered_table()
+        two.exchange_near()
     grad_first = arrived(back)
-    grad_field, gain_one, sums_one = backward(0, saved_first, grad_first, gain[0], w_qkv[0], w_proj[0], p_ref, gs_ref)
-    one.fill(weight_lanes([sums_one], gain_one))
+    grad_in, gain_one, weight_sums = backward(0, saved_first, grad_first, gain[0], w_qkv[0], w_proj[0], p_ref, gs_ref)
+    one.fill(weight_lanes([weight_sums()], gain_one))
     if alone:
         one.fill_table(reduce_lags(gs_ref, lag_ref))
         for sums, w_ref, t_ref in ((one, w_one, t_one), (two, w_two, t_two)):
@@ -497,13 +506,9 @@
             t_ref[...] = sums.t_src[...]
     else:
         one.scatter()
-        two.scattered()
-        two.exchange()
-        two.scattered_table()
-        two.exchange_near()
         one.fill_table(reduce_lags(gs_ref, lag_ref))
         one.scatter_table()
-    store_grid(field_ref, mm(from_rows, grad_field))
+    store_grid(field_ref, mm(from_rows, grad_in()))
     store_grid(out_ref, mm(from_rows, arrived(second)))
     if not alone:
         one.scattered()

time: 81.9 us -> 80.6 us (0.984)
  Pallas kernels: 81.1 us -> 79.8 us
    pallas_call x1, Pallas kernels: 78.5 us -> 77.2 us  [per_device(): pl.pallas_call(functools.partial(kernel, sizes), out_shape=[grid, grid] +...]
where the time goes in v4:
time: 80.6 us; the launch traced here: 80.4 us
  Pallas kernels  79.8 us (99%)
    pallas_call x1, Pallas kernels, per_device(): pl.pallas_call(functools.partial(kernel, sizes), out_shape=[grid, grid] +...  77.2 us
    pallas_call x1, Pallas kernels, per_device(): pl.pallas_call(functools.partial(finish, scale, table_scale), out_shape=[...  2.6 us

profile of v4, /device:TPU:1, one launch (start us, length us, event | category | flops | bytes accessed | tf_op | source)
XLA Modules:
  0.0 80.4 jit_solution(10354309213491119292)
XLA Ops:
  0.6 77.2 %shard_map.109 = (bf16[6,12,2,192]{3,2,1,0:T(2,128)(2,1)}, bf16[6,12,2,192]{3,2,1,0:T(2,128)(2,1)}, bf16[32,32,128]{2,1,0:T(8,128)(2,1)}, bf16[32,48,128]{2,1,0:...) custom-call(bf16[6,12,2,192]{3,2,1,0:T(2,128)(2,1)} %bitcast.7, bf16[6,12,2,192]{3,2,1,0:T(2,128)(2,1)} %bitcast.8, ...), custom_call_target="tpu_custom_call" | custom-call | tf_op jit(solution)/shard_map/pallas_call | solution.py:552
  77.9 2.6 %shard_map.110 = (bf16[6,12,2,192]{3,2,1,0:T(2,128)(2,1)}, bf16[6,12,2,192]{3,2,1,0:T(2,128)(2,1)}, f32[2,192]{1,0:T(2,128)}, f32[2,192,576]{2,1,0:T(8,128)}, f3...) custom-call(bf16[6,12,2,192]{3,2,1,0:T(2,128)(2,1)} %get-tuple-element.18.grid_a, ...), custom_call_target="tpu_custom_call" | custom-call | tf_op jit(solution)/shard_map/pallas_call | solution.py:582
